TPU v7x, 32 devices: a whole 2x2x4 slice. The times are simulated.
32 devices in a mesh: dp: 4 (over y, x), mp: 8 (over z, core).
Axes of the slice: x: 2, y: 2, z: 4, core: 2. Of those that a mesh axis runs over, the one named last changes fastest.
Arguments:
- features: bfloat16 [512, 16, 4096], P('mp', None, 'dp'), may hold values from -6 to 6
- styles: float32 [16, 512], P(None, 'mp'), may hold values from 0.3 to 8.5
- noise_field: bfloat16 [16, 4096], P(None, 'dp'), may hold values from -6 to 6
- noise_keep: int32 [16, 4096], P(None, 'dp'), may hold values 0 or 1
- path_noise: bfloat16 [3, 16, 4096], P(None, None, 'dp'), may hold values from -0.28125 to 0.28125
- length_mean: float32 [1], replicated, may hold values from 3 to 9
- conv_weight: float32 [512, 9, 512], P('mp'), may hold values from -4 to 4
- conv_moment: float32 [512, 9, 512], P('mp'), may hold values from -0.0007324219 to 0.0007324219
- conv_second: float32 [512, 9, 512], P('mp'), may hold values from 2.3841857e-09 to 9.536743e-09
- chan_params: float32 [2, 512], P(None, 'mp'), may hold values from -3 to 3
- chan_moment: float32 [2, 512], P(None, 'mp'), may hold values from -0.046875 to 0.046875
- chan_second: float32 [2, 512], P(None, 'mp'), may hold values from 8.583069e-06 to 3.4332275e-05
- rgb_weight: float32 [3, 512], P(None, 'mp'), may hold values from -18 to 18
- rgb_moment: float32 [3, 512], P(None, 'mp'), may hold values from -0.0234375 to 0.0234375
- rgb_second: float32 [3, 512], P(None, 'mp'), may hold values from 2.1457672e-06 to 8.583069e-06
Outputs:
- loss_sum: float32 [1], replicated
- clip_norm: float32 [1], replicated
- conv_moment_new: float32 [512, 9, 512], P('mp')
- conv_second_new: float32 [512, 9, 512], P('mp')
- conv_weight_new: float32 [512, 9, 512], P('mp')
- conv_weight_low: bfloat16 [512, 9, 512], P('mp')
- chan_moment_new: float32 [2, 512], P(None, 'mp')
- chan_second_new: float32 [2, 512], P(None, 'mp')
- chan_params_new: float32 [2, 512], P(None, 'mp')
- rgb_moment_new: float32 [3, 512], P(None, 'mp')
- rgb_second_new: float32 [3, 512], P(None, 'mp')
- rgb_weight_new: float32 [3, 512], P(None, 'mp')
- rgb_weight_low: bfloat16 [3, 512], P(None, 'mp')
All inputs are finite; a program needn't handle non-finite values. No bound on the sum of `noise_keep` on one device may be relied on, other than what follows from the above.
Results may differ from a plain program's by a relative error of at most 0.012.
Values may be sent and summed in bfloat16 or wider, within the bound.
A program may use at most 320 MiB of HBM per device.

v0:
```python
import math

import jax
import jax.numpy as jnp
from jax import lax
from jax.sharding import PartitionSpec as P

C = 512
SIDE = 64
STEP = 5


CLIP_LIMIT = 0.1
LEARN_RATE = 0.3
DECAY_RATE = 0.01
BETA_FIRST = 0.5
BETA_SECOND = 0.5
ADAM_EPSILON = 1e-08
DEMOD_EPSILON = 1e-08
HIGHEST = lax.Precision.HIGHEST


def extended(block, sides, width):
    for axis, dim in sides:
        count = lax.axis_size(axis)
        forward = [(i, i + 1) for i in range(count - 1)]
        backward = [(target, source) for source, target in forward]
        low = lax.ppermute(
            lax.slice_in_dim(block, block.shape[dim] - width, None, axis=dim), axis, forward
        )
        high = lax.ppermute(lax.slice_in_dim(block, 0, width, axis=dim), axis, backward)
        block = jnp.concatenate([low, block, high], axis=dim)
    return block


def adam_update(weight, moment, second, gradient, factor):
    clipped = gradient * factor
    moment_new = BETA_FIRST * moment + (1.0 - BETA_FIRST) * clipped
    second_new = BETA_SECOND * second + (1.0 - BETA_SECOND) * clipped * clipped
    moment_hat = moment_new / (1.0 - BETA_FIRST**STEP)
    second_hat = second_new / (1.0 - BETA_SECOND**STEP)
    weight_new = weight - LEARN_RATE * (
        moment_hat / (jnp.sqrt(second_hat) + ADAM_EPSILON) + DECAY_RATE * weight
    )
    return (moment_new, second_new, weight_new)


def tap_stack(padded):
    width = padded.shape[2] - 2 * SIDE - 2
    column = jnp.arange(width, dtype=jnp.int32) % SIDE
    stacked = []
    for vertical in range(3):
        for lateral in range(3):
            offset = vertical * SIDE + lateral
            window = padded[:, :, offset : offset + width]
            if lateral == 0:
                window = jnp.where(column >= 1, window, jnp.zeros_like(window))
            if lateral == 2:
                window = jnp.where(column <= SIDE - 2, window, jnp.zeros_like(window))
            stacked.append(window)
    return jnp.stack(stacked, axis=0)


def front(features, styles, weight_low, chan_use, noise_use):
    conv_gain = 1.0 / math.sqrt(9 * C)
    channels = weight_low.shape[0]
    modulated = (features.astype(jnp.float32) * styles.T[:, :, None]).astype(jnp.bfloat16)
    haloed = extended(modulated, (("dp", 2),), SIDE)
    haloed = jnp.pad(haloed, ((0, 0), (0, 0), (1, 1)))
    kept_input = tap_stack(haloed)
    summed = lax.psum_scatter(
        jnp.einsum("iko,kinp->onp", weight_low, kept_input, preferred_element_type=jnp.float32),
        "mp",
        scatter_dimension=0,
        tiled=True,
    )
    weight_float = weight_low.astype(jnp.float32)
    demod_part = jnp.dot(
        styles * styles, jnp.sum(weight_float * weight_float, axis=1), precision=HIGHEST
    )
    demod_all = lax.psum(demod_part, "mp")
    demod_sq = lax.dynamic_slice_in_dim(demod_all, lax.axis_index("mp") * channels, channels, 1)
    scaled = summed * conv_gain
    demod_scale = lax.rsqrt(conv_gain * conv_gain * demod_sq + DEMOD_EPSILON)
    pre_act = (
        scaled * demod_scale.T[:, :, None]
        + chan_use[1][:, None, None] * noise_use[None]
        + chan_use[0][:, None, None]
    )
    return (kept_input, scaled, demod_scale, pre_act)


def local(
    features,
    styles,
    noise_field,
    noise_keep,
    path_noise,
    length_mean,
    conv_weight,
    conv_moment,
    conv_second,
    chan_params,
    chan_moment,
    chan_second,
    rgb_weight,
    rgb_moment,
    rgb_second,
):
    conv_gain = 1.0 / math.sqrt(9 * C)
    rgb_gain = 1.0 / math.sqrt(C)
    channels = conv_weight.shape[0]
    weight_low = conv_weight.astype(jnp.bfloat16)
    rgb_low = rgb_weight.astype(jnp.bfloat16)
    noise_term = noise_field.astype(jnp.float32) * noise_keep.astype(jnp.float32)
    weight_use = weight_low.astype(jnp.float32)
    rgb_eff = rgb_low.astype(jnp.float32) * rgb_gain
    kept_input, scaled, demod_scale, pre_act = front(
        features, styles, weight_low, chan_params, noise_term
    )
    activated = jax.nn.silu(pre_act).astype(jnp.bfloat16)
    proj_part = jnp.einsum(
        "onp,cnp->noc", activated, path_noise, preferred_element_type=jnp.float32
    )
    projected = lax.psum(proj_part, "dp")
    path_slope = jnp.sum(projected * rgb_eff.T[None], axis=2)
    square_part = jnp.sum(path_slope * path_slope, axis=1)
    length_sq = lax.psum(square_part, "mp")
    length = jnp.sqrt(length_sq + 1e-08)
    excess = length - length_mean[0]
    loss_sum = jnp.sum(excess * excess)
    slope_grad = (2.0 * excess / length)[:, None] * path_slope
    rgb_term = rgb_gain * jnp.einsum("no,noc->co", slope_grad, projected, precision=HIGHEST)
    proj_grad = slope_grad[:, :, None] * rgb_eff.T[None]
    act_grad = jnp.einsum(
        "noc,cnp->onp", proj_grad, path_noise.astype(jnp.float32), precision=HIGHEST
    )
    kept_input, scaled, demod_scale, pre_act = front(
        features, styles, weight_low, chan_params, noise_term
    )
    sigmoid_value = jax.nn.sigmoid(pre_act)
    pre_grad = act_grad * sigmoid_value * (1.0 + pre_act * (1.0 - sigmoid_value))
    chan_term = jnp.stack(
        [jnp.sum(pre_grad, axis=(1, 2)), jnp.sum(pre_grad * noise_term[None], axis=(1, 2))]
    )
    demod_grad = jnp.sum(pre_grad * scaled, axis=2)
    stat_grad = demod_grad * (-0.5 * conv_gain * conv_gain) * demod_scale.T**3
    conv_grad = conv_gain * pre_grad * demod_scale.T[:, :, None]
    style_sq = styles * styles
    empty = jnp.zeros((channels, 9, C), jnp.float32)
    grad_piece = lax.all_gather(conv_grad.astype(jnp.bfloat16), "mp", axis=0, tiled=True)
    stat_piece = lax.all_gather(stat_grad.astype(jnp.bfloat16), "mp", axis=0, tiled=True).astype(
        jnp.float32
    )
    conv_term = jnp.einsum(
        "kinp,onp->iko", kept_input, grad_piece, preferred_element_type=jnp.float32
    )
    stat_cross = jnp.dot(style_sq.T, stat_piece.T, precision=HIGHEST)
    update = conv_term + 2.0 * weight_use * stat_cross[:, None, :]
    weight_part = lax.dynamic_update_slice_in_dim(empty, update, jnp.int32(0), 2)
    weight_grad, chan_grad = lax.psum((weight_part, chan_term), "dp")
    squares = (
        jnp.sum(weight_grad * weight_grad)
        + jnp.sum(chan_grad * chan_grad)
        + jnp.sum(rgb_term * rgb_term)
    )
    grad_norm = jnp.sqrt(lax.psum(squares, "mp"))
    factor = jnp.minimum(1.0, CLIP_LIMIT / (grad_norm + 1e-06))
    conv_m, conv_v, conv_new = adam_update(
        conv_weight, conv_moment, conv_second, weight_grad, factor
    )
    chan_m, chan_v, chan_new = adam_update(chan_params, chan_moment, chan_second, chan_grad, factor)
    rgb_m, rgb_v, rgb_new = adam_update(rgb_weight, rgb_moment, rgb_second, rgb_term, factor)
    return (
        loss_sum.reshape(1),
        grad_norm.reshape(1),
        conv_m,
        conv_v,
        conv_new,
        conv_new.astype(jnp.bfloat16),
        chan_m,
        chan_v,
        chan_new,
        rgb_m,
        rgb_v,
        rgb_new,
        rgb_new.astype(jnp.bfloat16),
    )


def solution(mesh):
    in_specs = (
        P("mp", None, "dp"),
        P(None, "mp"),
        P(None, "dp"),
        P(None, "dp"),
        P(None, None, "dp"),
        P(),
        P("mp", None, None),
        P("mp", None, None),
        P("mp", None, None),
        P(None, "mp"),
        P(None, "mp"),
        P(None, "mp"),
        P(None, "mp"),
        P(None, "mp"),
        P(None, "mp"),
    )
    out_specs = (
        P(),
        P(),
        P("mp", None, None),
        P("mp", None, None),
        P("mp", None, None),
        P("mp", None, None),
        P(None, "mp"),
        P(None, "mp"),
        P(None, "mp"),
        P(None, "mp"),
        P(None, "mp"),
        P(None, "mp"),
        P(None, "mp"),
    )
    return jax.shard_map(local, mesh=mesh, in_specs=in_specs, out_specs=out_specs, check_vma=False)
```

profile of v0, /device:TPU:0, one launch (start us, length us, event | category | flops | bytes accessed | tf_op | source)
XLA Modules:
  0.0 785.9 jit_solution(14782321767453973207)
XLA Ops:
  7.2 0.0 copy-start
  7.2 0.0 reduce-scatter.2.cloned.1.call-start
  7.2 3.1 multiply_convert_fusion.2
  10.3 0.2 fusion.66
  10.5 4.9 collective-permute-start
  15.3 1.3 collective-permute-start.1
  16.7 4.2 collective-permute-done
  20.9 7.6 collective-permute-done.1
  28.4 4.1 concatenate.14
  32.5 3.8 fusion.21
  36.3 2.6 fusion.18
  38.9 2.9 fusion.15
  41.8 2.8 fusion.29
  44.6 2.9 bitcast_dynamic-update-slice_fusion
  47.5 2.8 fusion.11
  50.3 2.8 fusion.7
  53.1 2.5 fusion.26
  55.5 2.5 fusion.24
  58.1 23.2 %convolution_bitcast_fusion = f32[512,16,1024]{0,2,1:T(8,128)} fusion(bf16[9,64,16,1024]{3,1,0,2:T(8,128)(2,1)} %fusion.24, f32[64,9,512]{2,0,1:T(8,128)S(1)} %copy-done.4), kind=kOutput, calls=%fused_computation.3 | convolution fusion | flops 9663971328 | bytes 53608448 | tf_op jit(solution)/shard_map/iko,kinp->onp/dot_general | solution.py:72
  81.3 33.1 %copy.68 = f32[512,16,1024]{2,1,0:T(8,128)} copy(f32[512,16,1024]{0,2,1:T(8,128)} %convolution_bitcast_fusion) | data formatting | bytes 67108864 | tf_op jit(solution)/shard_map/iko,kinp->onp/dot_general | solution.py:72
  114.4 0.0 reduce-scatter.2.cloned.1.call-update
  114.4 0.0 all-gather.3.cloned.1.call-start
  115.1 0.1 fusion.37
  115.2 0.2 fusion.48
  115.4 29.2 %psum.45 = f32[16,512]{1,0:T(8,128)S(1)} all-reduce(f32[16,512]{1,0:T(8,128)S(1)} %fusion.48), channel_id=1, replica_groups=mesh['dp'=4,'mp'=8] {'mp'}, use_global_device_ids=true, to_apply=%region_2.3 | all-reduce | flops 8192 | bytes 65536 | tf_op jit(solution)/shard_map/psum | solution.py:81
  144.6 0.1 bitcast_multiply_fusion.1
  144.7 296.3 %reduce-scatter.2.cloned.1.call-done = f32[64,16,1024]{2,1,0:T(8,128)} async-done(((f32[512,16,1024]{2,1,0:T(8,128)}), f32[64,16,1024]{2,1,0:T(8,128)}) %reduce-scatter.2.cloned.1.call-update) | async-done | bytes 4194320 | tf_op jit(solution)/shard_map/reduce_scatter | solution.py:71
  441.0 5.2 fusion.30
  446.2 16.0 %psum.46 = f32[16,64,3]{1,2,0:T(4,128)S(1)} all-reduce(f32[16,64,3]{1,2,0:T(4,128)S(1)} %fusion.30), channel_id=1, replica_groups=mesh['dp'=4,'mp'=8] {'dp'}, use_global_device_ids=true, to_apply=%region_3.4 | all-reduce | flops 3072 | bytes 24576 | tf_op jit(solution)/shard_map/psum | solution.py:125
  462.2 0.0 copy-start.6
  462.2 0.0 copy-start.9
  462.2 0.1 multiply_reduce_fusion.5
  462.3 13.6 %psum.47 = f32[16]{0:T(128)S(1)} all-reduce(f32[16]{0:T(128)S(1)} %multiply_reduce_fusion.5), channel_id=1, replica_groups=mesh['dp'=4,'mp'=8] {'mp'}, use_global_device_ids=true, to_apply=%region_6.7 | all-reduce | flops 16 | bytes 128 | tf_op jit(solution)/shard_map/psum | solution.py:128
  475.9 0.6 multiply_divide_fusion
  476.5 0.5 copy-done.15
  477.1 0.1 broadcast_multiply_fusion
  477.1 8.4 %fusion.60 = (f32[64]{0:T(128)}, f32[64]{0:T(128)}, f32[64,16]{0,1:T(8,128)S(1)}, bf16[64,16,1024]{2,0,1:T(8,128)(2,1)S(1)}) fusion(f32[16,1024]{1,0:T(8,128)S(1)} %convert_multiply_fusion.2, f32[64,16,1024]{2,1,0:T(8,128)} %reduce-scatter.2.cloned.1.call-done, f32[64,16]{0,1:T(8,128)S(1)} %bitcast_multiply_fusion.1, f32[64]{0:T(128)S(1)} %get-tuple-element.31, ...), kind=kOutput, calls=%fused_computation.110 | convolution fusion | flops 58722176 | bytes 6469376 | tf_op jit(solution)/shard_map/noc,cnp->onp/dot_general | solution.py:135
  485.5 2.5 copy.72
  488.0 0.0 all-gather.3.cloned.1.call-update
  488.0 0.0 all-reduce.3.cloned.1.call-start
  488.1 0.1 fusion.50
  488.2 14.0 %all-gather = bf16[8,64,16]{1,2,0:T(8,128)(2,1)S(1)} all-gather(bf16[1,64,16]{1,2,0:T(8,128)(2,1)S(1)} %fusion.50), channel_id=1, replica_groups=mesh['dp'=4,'mp'=8] {'mp'}, dimensions={0}, use_global_device_ids=true | all-gather | bytes 18432 | tf_op jit(solution)/shard_map/all_gather | solution.py:152
  502.2 0.1 reshape.60
  502.3 0.3 convolution_multiply_fusion
  502.6 133.3 %all-gather.3.cloned.1.call-done = bf16[512,16,1024]{2,1,0:T(8,128)(2,1)} async-done(((bf16[64,16,1024]{2,1,0:T(8,128)(2,1)}), bf16[512,16,1024]{2,1,0:T(8,128)(2,1)}) %all-gather.3.cloned.1.call-update) | async-done | bytes 16777232 | tf_op jit(solution)/shard_map/all_gather | solution.py:151
  635.9 0.0 copy-start.18
  635.9 0.0 copy-start.21
  635.9 0.0 copy-start.22
  635.9 0.0 copy-start.14
  636.0 0.0 copy-start.19
  636.0 0.0 copy-start.20
  636.0 61.9 %fusion.34 = f32[64,9,512]{2,0,1:T(8,128)} fusion(bf16[9,64,16,1024]{3,1,0,2:T(8,128)(2,1)} %fusion.24, bf16[512,16,1024]{2,1,0:T(8,128)(2,1)} %all-gather.3.cloned.1.call-done, f32[64,512]{1,0:T(8,128)S(1)} %convolution_multiply_fusion, f32[64,9,512]{2,0,1:T(8,128)S(1)} %copy-done.4), kind=kOutput, calls=%fused_computation.58 | convolution fusion | flops 9664856064 | bytes 38141952 | tf_op jit(solution)/shard_map/kinp,onp->iko/dot_general | solution.py:155
  697.9 0.0 all-reduce.3.cloned.1.call-update
  697.9 10.2 %psum.49 = f32[2,64]{1,0:T(2,128)S(1)} all-reduce(f32[2,64]{1,0:T(2,128)S(1)} %pad_maximum_fusion.2), channel_id=1, replica_groups=mesh['dp'=4,'mp'=8] {'dp'}, use_global_device_ids=true, to_apply=%region_13.14 | all-reduce | flops 128 | bytes 1024 | tf_op jit(solution)/shard_map/psum | solution.py:161
  708.1 0.6 multiply_reduce_fusion.7
  708.7 0.1 fusion.71
  708.8 0.6 multiply_reduce_fusion.6
  709.4 41.3 %all-reduce.3.cloned.1.call-done = f32[64,9,512]{2,0,1:T(8,128)} async-done(((f32[64,9,512]{2,0,1:T(8,128)}), f32[64,9,512]{2,0,1:T(8,128)}) %all-reduce.3.cloned.1.call-update) | async-done | bytes 1179664 | tf_op jit(solution)/shard_map/psum | solution.py:161
  750.8 2.2 multiply_reduce_fusion.2
  754.9 16.9 %psum.50 = f32[]{:T(128)} all-reduce(f32[]{:T(128)S(6)} %add.142), channel_id=1, replica_groups=mesh['dp'=4,'mp'=8] {'mp'}, use_global_device_ids=true, to_apply=%region_16.17 | all-reduce | flops 1 | bytes 8 | tf_op jit(solution)/shard_map/psum | solution.py:167
  772.5 0.6 multiply_subtract_fusion.2
  773.1 0.0 copy-start.1
  773.1 0.6 fusion.61
  773.7 4.3 fusion.64
  (48 shorter events, 0.2 us)
Async XLA Ops:
  7.2 433.9 %copy-start = (bf16[3,16,1024]{2,1,0:T(8,128)(2,1)S(1)}, bf16[3,16,1024]{2,1,0:T(8,128)(2,1)}, u32[]{:S(2)}) copy-start(bf16[3,16,1024]{2,1,0:T(8,128)(2,1)} %param.19) | copy-start | bytes 294916
  7.2 433.8 %reduce-scatter.2.cloned.1.call-start = ((), (), s32[]{:S(2)}) async-start(), calls=%async_computation.1 | async-start | bytes 37748736 | tf_op jit(solution)/shard_map/reduce_scatter | solution.py:71
  10.5 10.4 %collective-permute-start = (bf16[64,16,64]{2,0,1:T(8,128)(2,1)S(1)}, bf16[64,16,64]{2,0,1:T(8,128)(2,1)S(1)}, u32[]{:S(2)}, u32[]{:S(2)}) collective-permute-start(bf16[64,16,64]{2,0,1:T(8,128)(2,1)S(1)} %get-tuple-element.29), channel_id=1, source_target_pairs={{0,8},{8,16},{16,24},{1,9},{9,17},{17,25},{2,10},{10,18},{18,26},{... | collective-permute-start | bytes 393224 | tf_op jit(solution)/shard_map/ppermute | solution.py:28
  15.3 13.1 %collective-permute-start.1 = (bf16[64,16,64]{2,0,1:T(8,128)(2,1)S(1)}, bf16[64,16,64]{2,0,1:T(8,128)(2,1)S(1)}, u32[]{:S(2)}, u32[]{:S(2)}) collective-permute-start(bf16[64,16,64]{2,0,1:T(8,128)(2,1)S(1)} %get-tuple-element.28), channel_id=1, source_target_pairs={{8,0},{16,8},{24,16},{9,1},{17,9},{25,17},{10,2},{18,10},{26,18},{... | collective-permute-start | bytes 393224 | tf_op jit(solution)/shard_map/ppermute | solution.py:31
  41.8 2.8 copy-start.3
  41.8 2.8 copy-start.8
  53.1 2.5 copy-start.2
  55.5 2.5 copy-start.4
  114.4 30.3 %copy-start.17 = (f32[2,64]{1,0:T(2,128)S(1)}, f32[2,64]{1,0:T(2,128)}, u32[]{:S(2)}) copy-start(f32[2,64]{1,0:T(2,128)} %param.24) | copy-start | bytes 1540
  114.4 30.3 %copy-start.13 = (f32[3,64]{1,0:T(4,128)S(1)}, f32[3,64]{1,0:T(4,128)}, u32[]{:S(2)}) copy-start(f32[3,64]{1,0:T(4,128)} %param.27) | copy-start | bytes 2308
  114.4 30.3 %copy-start.11 = (s32[16,1024]{1,0:T(8,128)S(1)}, s32[16,1024]{1,0:T(8,128)}, u32[]{:S(2)}) copy-start(s32[16,1024]{1,0:T(8,128)} %param.18) | copy-start | bytes 196612
  114.4 30.3 %copy-start.12 = (bf16[16,1024]{1,0:T(8,128)(2,1)S(1)}, bf16[16,1024]{1,0:T(8,128)(2,1)}, u32[]{:S(2)}) copy-start(bf16[16,1024]{1,0:T(8,128)(2,1)} %param.17) | copy-start | bytes 98308
  114.4 521.5 %all-gather.3.cloned.1.call-start = ((), (), s32[]{:S(2)}) async-start(), calls=%async_computation.2 | async-start | bytes 18874368 | tf_op jit(solution)/shard_map/all_gather | solution.py:151
  462.2 23.3 %copy-start.6 = (f32[16,64,3]{1,2,0:T(4,128)}, f32[16,64,3]{1,2,0:T(4,128)S(1)}, u32[]{:S(2)}) copy-start(f32[16,64,3]{1,2,0:T(4,128)S(1)} %psum.46) | copy-start | bytes 36868
  462.2 23.3 %copy-start.9 = (f32[16,64]{1,0:T(8,128)}, f32[16,64]{1,0:T(8,128)S(1)}, u32[]{:S(2)}) copy-start(f32[16,64]{1,0:T(8,128)S(1)} %multiply_reduce_fusion.4) | copy-start | bytes 12292
  476.5 0.5 copy-start.15
  488.0 262.7 %all-reduce.3.cloned.1.call-start = ((), (), s32[]{:S(2)}) async-start(), calls=%async_computation.3 | async-start | bytes 2359296 | tf_op jit(solution)/shard_map/psum | solution.py:161
  635.9 62.0 %copy-start.23 = (f32[64]{0:T(128)S(1)}, f32[64]{0:T(128)}, u32[]{:S(2)}) copy-start(f32[64]{0:T(128)} %get-tuple-element.13) | copy-start | bytes 772
  635.9 62.0 %copy-start.24 = (f32[64]{0:T(128)S(1)}, f32[64]{0:T(128)}, u32[]{:S(2)}) copy-start(f32[64]{0:T(128)} %get-tuple-element.14) | copy-start | bytes 772
  635.9 72.8 %copy-start.10 = (f32[16,64]{1,0:T(8,128)S(1)}, f32[16,64]{1,0:T(8,128)}, u32[]{:S(2)}) copy-start(f32[16,64]{1,0:T(8,128)} %copy-done.9) | copy-start | bytes 12292
  635.9 72.8 %copy-start.16 = (f32[16]{0:T(128)S(1)}, f32[16]{0:T(128)}, u32[]{:S(2)}) copy-start(f32[16]{0:T(128)} %copy-done.15) | copy-start | bytes 196
  635.9 72.9 %copy-start.7 = (f32[16,64,3]{1,2,0:T(4,128)S(1)}, f32[16,64,3]{1,2,0:T(4,128)}, u32[]{:S(2)}) copy-start(f32[16,64,3]{1,2,0:T(4,128)} %copy-done.6) | copy-start | bytes 36868
  635.9 136.6 %copy-start.18 = (f32[2,64]{1,0:T(2,128)S(1)}, f32[2,64]{1,0:T(2,128)}, u32[]{:S(2)}) copy-start(f32[2,64]{1,0:T(2,128)} %param.24) | copy-start | bytes 1540
  635.9 136.6 %copy-start.21 = (f32[2,64]{1,0:T(2,128)S(1)}, f32[2,64]{1,0:T(2,128)}, u32[]{:S(2)}) copy-start(f32[2,64]{1,0:T(2,128)} %param.26) | copy-start | bytes 1540
  635.9 136.6 %copy-start.22 = (f32[2,64]{1,0:T(2,128)S(1)}, f32[2,64]{1,0:T(2,128)}, u32[]{:S(2)}) copy-start(f32[2,64]{1,0:T(2,128)} %param.25) | copy-start | bytes 1540
  635.9 137.2 %copy-start.14 = (f32[3,64]{1,0:T(4,128)S(1)}, f32[3,64]{1,0:T(4,128)}, u32[]{:S(2)}) copy-start(f32[3,64]{1,0:T(4,128)} %param.27) | copy-start | bytes 2308
  636.0 137.2 %copy-start.19 = (f32[3,64]{1,0:T(4,128)S(1)}, f32[3,64]{1,0:T(4,128)}, u32[]{:S(2)}) copy-start(f32[3,64]{1,0:T(4,128)} %param.29) | copy-start | bytes 2308
  636.0 137.1 %copy-start.20 = (f32[3,64]{1,0:T(4,128)S(1)}, f32[3,64]{1,0:T(4,128)}, u32[]{:S(2)}) copy-start(f32[3,64]{1,0:T(4,128)} %param.28) | copy-start | bytes 2308
  697.9 75.9 %copy-start.5 = (f32[64,9,512]{2,0,1:T(8,128)S(1)}, f32[64,9,512]{2,0,1:T(8,128)}, u32[]{:S(2)}) copy-start(f32[64,9,512]{2,0,1:T(8,128)} %param.23) | copy-start | bytes 3538948
  773.1 5.0 copy-start.1
Sparse Core Ops, SparseCore 0:
  114.5 326.4 reduce-scatter.1
  488.2 147.6 all-gather.2
  698.0 52.6 all-reduce.2
where the time goes:
time: 789 us; the launch traced here: 786 us
  waiting for transfers between devices  483 us (61%)
  blocking collectives  99.8 us (13%)
  matrix products  99.1 us (13%)
  local copies, waits for them, and re-layouts  40.5 us (5%)
  other arithmetic  38.8 us (5%)
  between operations  18.7 us (2%)
    reduce_scatter x1, waiting for transfers between devices, front(): lax.psum_scatter(jnp.einsum('iko,kinp->onp', weight_low, kept_input, pref...  296 us
    all_gather x1, waiting for transfers between devices, local(): lax.all_gather(conv_grad.astype(jnp.bfloat16), 'mp', axis=0, tiled=True)  133 us
    dot_general x1, matrix products, local(): jnp.einsum('kinp,onp->iko', kept_input, grad_piece, preferred_element_typ...  61.9 us
    psum x1, waiting for transfers between devices, local(): weight_grad, chan_grad = lax.psum((weight_part, chan_term), 'dp')  41.3 us
    dot_general x1, local copies, waits for them, and re-layouts, front(): jnp.einsum('iko,kinp->onp', weight_low, kept_input, preferred_element_typ...  33.1 us
    psum x1, blocking collectives, front(): demod_all = lax.psum(demod_part, 'mp')  29.2 us
    dot_general x1, matrix products, front(): jnp.einsum('iko,kinp->onp', weight_low, kept_input, preferred_element_typ...  23.2 us
    unnamed x10, other arithmetic  23.2 us
  transfers between devices with their start and end apart: 5, of which 5 were waited for; matrix products, arithmetic and copies ran while one was open for 0% of the time, Pallas kernels for 0%

commit v1 on v0

v1 whole, which is shorter than its diff:
```python
import functools
import math

import jax
import jax.numpy as jnp
from jax import lax
from jax.experimental import pallas as pl
from jax.experimental.pallas import tpu as pltpu
from jax.sharding import PartitionSpec as P

SIDE = 64
STEP = 5
TAPS = 9
LANES = 128

CLIP_LIMIT = 0.1
LEARN_RATE = 0.3
DECAY_RATE = 0.01
BETA_FIRST = 0.5
BETA_SECOND = 0.5
ADAM_EPSILON = 1e-08
DEMOD_EPSILON = 1e-08
HIGHEST = lax.Precision.HIGHEST
MESH = pl.DeviceIdType.MESH
F32 = jnp.float32
BF16 = jnp.bfloat16
NT = (((1,), (1,)), ((), ()))


class Sizes:
    def __init__(self, mesh_shape, features, conv_weight):
        self.dp = mesh_shape["dp"]
        self.mp = mesh_shape["mp"]
        self.chips = self.mp // 2
        self.ch, self.images, self.px = features
        self.width = conv_weight[2]
        self.half = self.width // 2
        self.group = self.images // self.chips
        self.blocks = self.px // LANES
        self.ext = self.px + 2 * LANES
        self.split = (self.ch // self.dp) % 16 == 0
        self.shares = self.dp if self.split else 1
        self.rows = self.ch // self.shares
        self.taps_each = 3


def flip(value, bit):
    return value + bit - 2 * bit * lax.rem(lax.div(value, bit), 2)


def swap_halves(x):
    return pltpu.roll(x, SIDE, x.ndim - 1)


def kernel(
    s,
    feat_hbm,
    styles,
    weight_hbm,
    pack,
    aux_hbm,
    mean,
    grad_out,
    small_out,
    norm_out,
    feat,
    turned,
    outbox,
    grids,
    weight_own,
    weight_low,
    weights,
    weights_t,
    weight_sq,
    pack_all,
    columns,
    rgb_rows,
    demod_rows,
    demod_cols,
    chan_cols,
    aux,
    halo_out,
    halo_in,
    scaled,
    slope_of,
    proj_all,
    half_pick,
    stat_rows,
    rgb_acc,
    loss_acc,
    chan_acc,
    grad_conv,
    total,
    share_out,
    share_in,
    line_out,
    line_in,
    final,
    gathered,
    small_own,
    small_plane,
    small_mid,
    small_line,
    square_all,
    in_sem,
    w_send,
    w_recv,
    w_plane_send,
    w_plane_recv,
    p_send,
    p_recv,
    f_send,
    f_recv,
    f_local,
    f_swap,
    h_send,
    h_recv,
    j_send,
    j_recv,
    r_send,
    r_recv,
    l_send,
    l_recv,
    g_send,
    g_recv,
    sp_send,
    sp_recv,
    sl_send,
    sl_recv,
    n_send,
    n_recv,
):
    d = lax.axis_index("dp")
    m = lax.axis_index("mp")
    z = lax.div(m, 2)
    c = lax.rem(m, 2)
    other = 1 - c
    mate = 2 * z + other
    conv_gain = 1.0 / math.sqrt(TAPS * s.width)
    rgb_gain = 1.0 / math.sqrt(s.width)
    last = s.group - 1

    def copy_to(src, dst, send, recv, dd, mm):
        return pltpu.make_async_remote_copy(
            src_ref=src, dst_ref=dst, send_sem=send, recv_sem=recv, device_id=(dd, mm), device_id_type=MESH
        )

    def z_at(r):
        return lax.rem(z + r, s.chips)

    def d_at(r):
        return lax.rem(d + r, s.dp)

    line = [(d, lax.rem(m + r, s.mp)) for r in range(1, s.mp)]
    plane = [(d_at(r), mm) for r in range(1, s.dp) for mm in (m, mate)]
    near = plane + [(d, mate)]

    get_weight = pltpu.make_async_copy(weight_hbm, weight_own, in_sem.at[0])
    get_feat = pltpu.make_async_copy(feat_hbm, feat, in_sem.at[1])
    get_aux = pltpu.make_async_copy(aux_hbm.at[pl.ds(z * s.group, s.group)], aux, in_sem.at[2])
    get_weight.start()
    get_feat.start()
    get_aux.start()
    halo_in[...] = jnp.zeros_like(halo_in)
    barrier = pltpu.get_barrier_semaphore()
    for dd, mm in line + plane:
        pl.semaphore_signal(barrier, inc=1, device_id=(dd, mm), device_id_type=MESH)

    get_weight.wait()
    for k in range(TAPS):
        weight_low[k] = weight_own[k].astype(BF16)
    weights[:, pl.ds(pl.multiple_of(m * s.ch, 16), s.ch), :] = weight_low[
        :, :, pl.ds(pl.multiple_of(c * s.half, LANES), s.half)
    ]
    pl.semaphore_wait(barrier, len(line) + len(plane))

    share = d if s.split else 0
    piece_rows = s.rows

    def piece(m_of):
        return pl.ds(pl.multiple_of(m_of * s.ch + share * piece_rows, 16), piece_rows)

    def own_piece(half_of):
        return weight_low.at[
            :,
            pl.ds(pl.multiple_of(share * piece_rows, 16), piece_rows),
            pl.ds(pl.multiple_of(half_of * s.half, LANES), s.half),
        ]

    mate_rows = pl.ds(pl.multiple_of(m * s.ch, 16), s.ch)
    sends = []
    to_mate = copy_to(
        weight_low.at[:, :, pl.ds(pl.multiple_of(other * s.half, LANES), s.half)],
        weights.at[:, mate_rows, :],
        w_send.at[0],
        w_recv.at[m],
        d,
        mate,
    )
    to_mate.start()
    sends.append(to_mate)
    bits = []
    bit = s.chips // 2
    while bit >= 1:
        bits.append(bit)
        bit //= 2
    count = 1
    for bit in bits:
        for cc in range(2):
            cp = copy_to(
                own_piece(cc), weights.at[:, piece(m), :], w_send.at[count], w_recv.at[m], d, 2 * flip(z, bit) + cc
            )
            cp.start()
            sends.append(cp)
            count += 1
    for r, (dd, mm) in enumerate(line):
        cp = copy_to(pack.at[lax.div(mm, 2)], pack_all.at[m], p_send.at[r], p_recv.at[m], dd, mm)
        cp.start()
        sends.append(cp)
    pack_all[m] = pack[z]

    get_feat.wait()
    lane = lax.broadcasted_iota(jnp.int32, (1, 1, LANES), 2)
    low_lanes = lane < SIDE
    step = 8

    def modulate(index, carry):
        rows = pl.ds(pl.multiple_of(index * step, step), step)
        factor = styles[rows]
        for q in range(s.blocks // 2):
            first = feat[rows, :, q * LANES : (q + 1) * LANES].astype(F32) * factor
            q2 = q + s.blocks // 2
            second = feat[rows, :, q2 * LANES : (q2 + 1) * LANES].astype(F32) * factor
            even = jnp.where(low_lanes, first, swap_halves(second))
            odd = jnp.where(low_lanes, swap_halves(first), second)
            out_rows = pl.ds(pl.multiple_of(index * step * s.images, step * 8), step * s.images)
            turned[2 * q, out_rows, :] = even.reshape(step * s.images, LANES)
            turned[2 * q + 1, out_rows, :] = odd.reshape(step * s.images, LANES)
        return carry

    lax.fori_loop(0, s.ch // step, modulate, 0)

    def pick(n, carry):
        for j in range(s.blocks):
            part = turned[j, pl.ds(n, s.ch, stride=s.images), :]
            outbox[n, :, j * LANES : (j + 1) * LANES] = part.astype(BF16)
        return carry

    lax.fori_loop(0, s.images, pick, 0)

    middle = pl.ds(LANES, s.px)

    def grid_rows(m_of):
        return pl.ds(pl.multiple_of(m_of * s.ch, 16), s.ch)

    def feature_send(q, r):
        zz = z_at(r)
        return copy_to(
            outbox.at[zz * s.group + q],
            grids.at[q, 1, grid_rows(m), middle],
            f_send.at[q, r],
            f_recv.at[q, m],
            d,
            2 * zz + c,
        )

    def own_to_mate(q):
        return copy_to(
            outbox.at[z * s.group + q],
            grids.at[q, 1, grid_rows(m), middle],
            f_send.at[q, 0],
            f_recv.at[q, m],
            d,
            mate,
        )

    def own_local(q):
        return pltpu.make_async_copy(
            outbox.at[z * s.group + q], grids.at[q, 1, grid_rows(m), middle], f_local.at[q]
        )

    def swap_send(q, r):
        rows = grid_rows(2 * z_at(r) + c)
        return copy_to(
            grids.at[q, 1, rows, middle],
            grids.at[q, 1, rows, middle],
            f_swap.at[q, r],
            f_recv.at[q, 2 * z_at(r) + c],
            d,
            mate,
        )

    for q in range(s.group):
        own_local(q).start()
        own_to_mate(q).start()
    for q in range(2):
        for r in range(1, s.chips):
            feature_send(q, r).start()

    held = [z]
    for index, bit in enumerate(bits):
        peer = flip(z, bit)
        for h in held[1:]:
            for cc in range(2):
                cp = copy_to(
                    weights.at[:, piece(2 * h + cc), :],
                    weights.at[:, piece(2 * h + cc), :],
                    w_send.at[count],
                    w_recv.at[2 * h + cc],
                    d,
                    2 * peer + c,
                )
                cp.start()
                sends.append(cp)
                count += 1
        fresh = [flip(h, bit) for h in held]
        for h in fresh:
            for cc in range(2):
                mm = 2 * h + cc
                copy_to(
                    weights.at[:, piece(mm), :], weights.at[:, piece(mm), :], w_send.at[0], w_recv.at[mm], d, mate
                ).wait_recv()
                if s.split:
                    for r in range(1, s.dp):
                        cp = copy_to(
                            weights.at[:, piece(mm), :],
                            weights.at[:, piece(mm), :],
                            w_plane_send.at[r, mm],
                            w_plane_recv.at[r, mm],
                            d_at(r),
                            m,
                        )
                        cp.start()
                        sends.append(cp)
        held = held + fresh

    for dd, mm in line:
        copy_to(pack.at[0], pack_all.at[mm], p_send.at[0], p_recv.at[mm], d, mate).wait_recv()
    for mm in range(s.mp):
        columns[mm * s.ch : (mm + 1) * s.ch, :] = pack_all[mm].T[: s.ch, :]
    rows_all = columns[...].T
    for h in range(2):
        rgb_rows[h] = rows_all[8:16, h * s.half : (h + 1) * s.half]
    mine = columns[pl.ds(pl.multiple_of(c * s.half, 8), s.half), :]
    for k in range(2):
        chan_cols[k] = jnp.broadcast_to(mine[:, s.group + k : s.group + k + 1], (s.half, LANES))
    total[...] = jnp.zeros_like(total)
    stat_rows[...] = jnp.zeros_like(stat_rows)
    rgb_acc[...] = jnp.zeros_like(rgb_acc)
    loss_acc[...] = jnp.zeros_like(loss_acc)
    chan_acc[...] = jnp.zeros_like(chan_acc)

    copy_to(weights.at[:, mate_rows, :], weights.at[:, mate_rows, :], w_send.at[0], w_recv.at[mate], d, mate).wait_recv()
    if s.split:
        for h in held[1:]:
            for cc in range(2):
                mm = 2 * h + cc
                for r in range(1, s.dp):
                    copy_to(
                        weights.at[:, piece(mm), :],
                        weights.at[:, piece(mm), :],
                        w_plane_send.at[r, mm],
                        w_plane_recv.at[r, mm],
                        d,
                        mate,
                    ).wait_recv()
    square = jnp.zeros((s.width, s.half), F32)
    for k in range(TAPS):
        w = weights[k]
        weights_t[:, k * s.width : (k + 1) * s.width] = w.T
        wf = w.astype(F32)
        square = square + wf * wf
    weight_sq[...] = square
    demod_sq = jnp.dot(rows_all * rows_all, weight_sq[...], precision=HIGHEST, preferred_element_type=F32)
    demod = lax.rsqrt(conv_gain * conv_gain * demod_sq + DEMOD_EPSILON)
    demod_rows[...] = demod
    demod_t = demod.T
    for q in range(s.group):
        demod_cols[q] = jnp.broadcast_to(demod_t[:, q : q + 1], (s.half, LANES))
    get_aux.wait()

    lane2 = lax.broadcasted_iota(jnp.int32, (1, LANES), 1)
    low2 = lane2 < SIDE
    column = lax.rem(lane2, SIDE)
    not_first = column >= 1
    not_last = column <= SIDE - 2
    pair = s.width // 2
    up = lax.rem(d + s.dp - 1, s.dp)
    down = lax.rem(d + 1, s.dp)

    def halo_up(q):
        return copy_to(halo_out.at[q, 0], halo_in.at[q, 1], h_send.at[q, 0], h_recv.at[q, 1], up, m)

    def halo_down(q):
        return copy_to(halo_out.at[q, 1], halo_in.at[q, 0], h_send.at[q, 1], h_recv.at[q, 0], down, m)

    place = 2 * d + c

    def proj_send(q, index):
        dd, mm = near[index]
        return copy_to(
            proj_all.at[q, place],
            proj_all.at[q, place],
            j_send.at[q, index],
            j_recv.at[q, place],
            dd,
            mm,
        )

    def forward(q):
        for r in range(1, s.chips):
            mm = 2 * z_at(r) + c
            rows = grid_rows(mm)
            copy_to(
                grids.at[q, 1, rows, middle], grids.at[q, 1, rows, middle], f_swap.at[q, r], f_recv.at[q, mm], d, mate
            ).wait_recv()
            swap_send(q, r).start()

        @pl.when(q + 2 < s.group)
        def _():
            for r in range(1, s.chips):
                feature_send(q + 2, r).start()

        own_local(q).wait()
        for r in range(s.chips):
            mm = 2 * z_at(r) + other
            rows = grid_rows(mm)
            copy_to(
                grids.at[q, 1, rows, middle], grids.at[q, 1, rows, middle], f_swap.at[q, 0], f_recv.at[q, mm], d, mate
            ).wait_recv()
        top = grids[q, 1, :, LANES : 2 * LANES]
        end = grids[q, 1, :, s.px : s.px + LANES]
        halo_out[q, 0] = jnp.where(low2, top[:pair], swap_halves(top[pair:]))
        halo_out[q, 1] = jnp.where(low2, swap_halves(end[:pair]), end[pair:])

        @pl.when(d > 0)
        def _():
            halo_up(q).start()

        @pl.when(d < s.dp - 1)
        def _():
            halo_down(q).start()

        def lateral(j):
            x = grids[q, 1, :, j * LANES : (j + 1) * LANES]
            none = jnp.zeros_like(x)
            grids[q, 0, :, j * LANES : (j + 1) * LANES] = jnp.where(not_first, pltpu.roll(x, 1, 1), none)
            grids[q, 2, :, j * LANES : (j + 1) * LANES] = jnp.where(not_last, pltpu.roll(x, LANES - 1, 1), none)

        for j in range(1, s.blocks + 1):
            lateral(j)

        @pl.when(d > 0)
        def _():
            halo_down(q).wait_recv()

        @pl.when(d < s.dp - 1)
        def _():
            halo_up(q).wait_recv()

        above = halo_in[q, 0]
        below = halo_in[q, 1]
        swapped_end = swap_halves(end)
        swapped_top = swap_halves(top)
        grids[q, 1, :pair, :LANES] = jnp.where(low2, above, swapped_end[:pair])
        grids[q, 1, pair:, :LANES] = jnp.where(low2, swap_halves(above), swapped_end[pair:])
        tail = s.px + LANES
        grids[q, 1, :pair, tail : tail + LANES] = jnp.where(low2, swapped_top[:pair], swap_halves(below))
        grids[q, 1, pair:, tail : tail + LANES] = jnp.where(low2, swapped_top[pair:], below)
        lateral(0)
        lateral(s.blocks + 1)

        projected = jnp.zeros((16, s.half), F32)
        wide = 2 * LANES
        for p in range(0, s.px, wide):
            acc = jnp.zeros((s.half, wide), F32)
            for a in range(3):
                for b in range(3):
                    k = 3 * a + b
                    acc += jnp.dot(
                        weights_t[:, k * s.width : (k + 1) * s.width],
                        grids[q, b, :, a * LANES + p : a * LANES + p + wide],
                        preferred_element_type=F32,
                    )
            acts = []
            for t in range(2):
                cut = slice(p + t * LANES, p + (t + 1) * LANES)
                conv = acc[:, t * LANES : (t + 1) * LANES] * conv_gain
                noise = aux[q, :, cut].astype(F32)[3:4]
                pre = conv * demod_cols[q] + chan_cols[1] * noise + chan_cols[0]
                sig = jax.nn.sigmoid(pre)
                act = pre * sig
                scaled[q, :, cut] = conv
                slope_of[q, :, cut] = sig * (1.0 + pre * (1.0 - sig))
                acts.append(act.astype(BF16))
            act = jnp.concatenate(acts, axis=1)
            projected += lax.dot_general(aux[q, :, p : p + wide], act, NT, preferred_element_type=F32)
        proj_all[q, place] = projected[:8]
        for index in range(len(near)):
            proj_send(q, index).start()

    def signal_back(q):
        for r in range(1, 2 * s.dp):
            at = lax.rem(place + r, 2 * s.dp)
            copy_to(
                proj_all.at[q, at], proj_all.at[q, at], j_send.at[q, 0], j_recv.at[q, at], d, mate
            ).wait_recv()
        halves = []
        for h in range(2):
            acc = proj_all[q, h]
            for dd in range(1, s.dp):
                acc = acc + proj_all[q, 2 * dd + h]
            halves.append(acc)
        slopes = [jnp.sum(rgb_rows[h] * halves[h], axis=0, keepdims=True) for h in range(2)]
        row = lax.broadcasted_iota(jnp.int32, (8, s.half), 0)
        length_sq = jnp.sum(slopes[0] * slopes[0] + slopes[1] * slopes[1], axis=1, keepdims=True)
        length = jnp.sqrt(length_sq + 1e-08)
        excess = length - mean[0]
        loss_acc[...] += jnp.broadcast_to(excess * excess, (1, s.half))
        scale = 2.0 * excess / length
        for h in range(2):
            grad = scale * slopes[h]
            half_pick[h, 0] = grad * rgb_rows[h]
            half_pick[h, 1] = jnp.where(row < 3, grad * halves[h] * rgb_gain, 0.0)
        rgb_acc[...] += half_pick[c, 1]
        coef = half_pick[c, 0]
        high = coef.astype(BF16).astype(F32)
        coef_t = jnp.concatenate([high, coef - high], axis=0).T.astype(BF16)
        wide = 2 * LANES
        bias_part = chan_acc[0]
        strength_part = chan_acc[1]
        stat_part = jnp.zeros((s.half, LANES), F32)
        back = demod_cols[q] * conv_gain
        for p in range(0, s.px, wide):
            act_grad = jnp.dot(coef_t, aux[q, :, p : p + wide], preferred_element_type=F32)
            for t in range(2):
                cut = slice(p + t * LANES, p + (t + 1) * LANES)
                noise = aux[q, :, cut].astype(F32)[3:4]
                grad = act_grad[:, t * LANES : (t + 1) * LANES] * slope_of[q, :, cut]
                bias_part = bias_part + grad
                strength_part = strength_part + grad * noise
                stat_part = stat_part + grad * scaled[q, :, cut]
                grad_conv[:, cut] = (grad * back).astype(BF16)
        chan_acc[0] = bias_part
        chan_acc[1] = strength_part
        stat = jnp.sum(stat_part.T, axis=0, keepdims=True)
        dem = demod_rows[pl.ds(q, 1), :]
        stat_rows[pl.ds(q, 1), :] = stat * (dem * dem * dem) * (-0.5 * conv_gain * conv_gain)

    def tap_grad(q, k):
        a, b = k // 3, k % 3
        return lax.dot_general(
            grids[q, b, :, a * LANES : a * LANES + s.px], grad_conv[...], NT, preferred_element_type=F32
        )

    def stage(q, carry):
        forward(q)

        @pl.when(q > 0)
        def _():
            signal_back(q - 1)
            for k in range(TAPS):
                total[k] += tap_grad(q - 1, k)

        return carry

    lax.fori_loop(0, s.group, stage, 0)

    signal_back(last)
    small_own[0:1] = jnp.sum(chan_acc[0].T, axis=0, keepdims=True)
    small_own[1:2] = jnp.sum(chan_acc[1].T, axis=0, keepdims=True)
    small_own[2:3] = loss_acc[...]
    small_own[3:8] = jnp.zeros((5, s.half), F32)
    small_own[8:16] = rgb_acc[...]
    small_plane[place] = small_own[...]
    for index, (dd, mm) in enumerate(near):
        cp = copy_to(small_own, small_plane.at[place], sp_send.at[index], sp_recv.at[place], dd, mm)
        cp.start()
        sends.append(cp)
    cross = 2.0 * jnp.dot(
        columns[...] * columns[...], stat_rows[...], precision=HIGHEST, preferred_element_type=F32
    )
    weight_sq[...] = cross

    def share_part(k, share_of):
        return share_out.at[k, :, pl.ds(pl.multiple_of(share_of * s.rows, 16), s.rows), :]

    for k in range(TAPS):
        grad = total[k] + tap_grad(last, k) + weights[k].astype(F32) * weight_sq[...]
        share_out[k] = grad.astype(BF16).reshape(s.mp, s.ch, s.half)
        for r in range(1, s.dp):
            cp = copy_to(
                share_part(k, d_at(r) if s.split else 0),
                share_in.at[d, k],
                r_send.at[r, k],
                r_recv.at[d, k],
                d_at(r),
                m,
            )
            cp.start()
            sends.append(cp)

    for r in range(1, 2 * s.dp):
        at = lax.rem(place + r, 2 * s.dp)
        copy_to(small_own, small_plane.at[at], sp_send.at[0], sp_recv.at[at], d, mate).wait_recv()
    for h in range(2):
        acc = small_plane[h, 0:8]
        for dd in range(1, s.dp):
            acc = acc + small_plane[2 * dd + h, 0:8]
        row = lax.broadcasted_iota(jnp.int32, (8, s.half), 0)
        small_mid[h, 0:8] = jnp.where(row < 2, acc, small_plane[h, 0:8])
        small_mid[h, 8:16] = small_plane[h, 8:16]
    small_line[z] = small_mid[...]
    for r in range(1, s.chips):
        cp = copy_to(small_mid, small_line.at[z], sl_send.at[r], sl_recv.at[z], d, 2 * z_at(r) + c)
        cp.start()
        sends.append(cp)

    groups = TAPS // s.taps_each
    for g in range(groups):
        for k in range(g * s.taps_each, (g + 1) * s.taps_each):
            for r in range(1, s.dp):
                copy_to(
                    share_in.at[d_at(r), k], share_in.at[d_at(r), k], r_send.at[r, k], r_recv.at[d_at(r), k], d, mate
                ).wait_recv()
            own = share_out[k, :, pl.ds(pl.multiple_of(share * s.rows, 16), s.rows), :].astype(F32)
            acc = None
            for dd in range(s.dp):
                term = jnp.where(d == dd, own, share_in[dd, k].astype(F32))
                acc = term if acc is None else acc + term
            line_out[:, k] = acc.astype(BF16).reshape(s.chips, 2, s.rows, s.half)
        taps = pl.ds(g * s.taps_each, s.taps_each)
        for r in range(1, s.chips):
            cp = copy_to(
                line_out.at[z_at(r), taps], line_in.at[r, taps], l_send.at[r, g], l_recv.at[r, g], d, 2 * z_at(r) + c
            )
            cp.start()
            sends.append(cp)
    own_rows = pl.ds(pl.multiple_of(share * s.rows, 16), s.rows)
    own_cols = pl.ds(pl.multiple_of(c * s.half, LANES), s.half)
    targets = near if s.split else [(d, mate)]
    for g in range(groups):
        taps = pl.ds(g * s.taps_each, s.taps_each)
        for r in range(1, s.chips):
            copy_to(line_out.at[0, taps], line_in.at[r, taps], l_send.at[r, g], l_recv.at[r, g], d, mate).wait_recv()
        for k in range(g * s.taps_each, (g + 1) * s.taps_each):
            acc = line_out[z, k].astype(F32)
            for r in range(1, s.chips):
                acc = acc + line_in[r, k].astype(F32)
            final[:, k] = acc.astype(BF16)
            gathered[k, own_rows, own_cols] = final[c, k]
        for index, (dd, mm) in enumerate(targets):
            cp = copy_to(
                final.at[lax.rem(mm, 2), taps],
                gathered.at[taps, own_rows, own_cols],
                g_send.at[index, g],
                g_recv.at[place, g],
                dd,
                mm,
            )
            cp.start()
            sends.append(cp)
    for r in range(1, s.chips):
        copy_to(small_mid, small_line.at[z_at(r)], sl_send.at[r], sl_recv.at[z_at(r)], d, mate).wait_recv()
    sums = small_line[0]
    for zz in range(1, s.chips):
        sums = sums + small_line[zz]
    small_out[...] = sums
    chan_squares = jnp.sum(sums[:, 0:2] * sums[:, 0:2]) + jnp.sum(sums[:, 8:16] * sums[:, 8:16])

    for g in range(groups):
        taps = pl.ds(g * s.taps_each, s.taps_each)
        if s.split:
            for r in range(1, 2 * s.dp):
                at = lax.rem(place + r, 2 * s.dp)
                rows = pl.ds(pl.multiple_of(lax.div(at, 2) * s.rows, 16), s.rows)
                cols = pl.ds(pl.multiple_of(lax.rem(at, 2) * s.half, LANES), s.half)
                copy_to(
                    final.at[0, taps], gathered.at[taps, rows, cols], g_send.at[0, g], g_recv.at[at, g], d, mate
                ).wait_recv()
        else:
            cols = pl.ds(pl.multiple_of(other * s.half, LANES), s.half)
            copy_to(
                final.at[0, taps], gathered.at[taps, own_rows, cols], g_send.at[0, g], g_recv.at[2 * d + other, g], d, mate
            ).wait_recv()
    acc = jnp.zeros((s.ch, s.width), F32)
    for k in range(TAPS):
        grad = gathered[k].astype(F32)
        acc = acc + grad * grad
    square_all[m] = jnp.broadcast_to(jnp.sum(acc, keepdims=True), (8, LANES))
    for index, (dd, mm) in enumerate(line):
        cp = copy_to(square_all.at[m], square_all.at[m], n_send.at[index], n_recv.at[m], dd, mm)
        cp.start()
        sends.append(cp)
    grad_out[...] = gathered[...]
    for dd, mm in line:
        copy_to(square_all.at[mm], square_all.at[mm], n_send.at[0], n_recv.at[mm], d, mate).wait_recv()
    acc = square_all[0]
    for mm in range(1, s.mp):
        acc = acc + square_all[mm]
    norm_out[...] = jnp.sqrt(acc + chan_squares)

    for cp in sends:
        cp.wait_send()

    def settle(q, carry):
        for r in range(1, s.chips):
            feature_send(q, r).wait_send()
            swap_send(q, r).wait_send()
        own_to_mate(q).wait_send()
        for index in range(len(near)):
            proj_send(q, index).wait_send()

        @pl.when(d > 0)
        def _():
            halo_up(q).wait_send()

        @pl.when(d < s.dp - 1)
        def _():
            halo_down(q).wait_send()

        return carry

    lax.fori_loop(0, s.group, settle, 0)


def run_kernel(s, feat, styles, weight, pack, aux, mean):
    vm, dma = pltpu.VMEM, pltpu.SemaphoreType.DMA
    bits = int(math.log2(s.chips))
    near = 2 * s.dp - 1
    groups = TAPS // s.taps_each
    scratch = [
        vm((s.ch, s.images, s.px), BF16),
        vm((s.blocks, s.ch * s.images, LANES), F32),
        vm((s.images, s.ch, s.px), BF16),
        vm((s.group, 3, s.width, s.ext), BF16),
        vm((TAPS, s.ch, s.width), F32),
        vm((TAPS, s.ch, s.width), BF16),
        vm((TAPS, s.width, s.half), BF16),
        vm((s.half, TAPS * s.width), BF16),
        vm((s.width, s.half), F32),
        vm((s.mp, 16, LANES), F32),
        vm((s.width, 16), F32),
        vm((2, 8, s.half), F32),
        vm((16, s.half), F32),
        vm((s.group, s.half, LANES), F32),
        vm((2, s.half, LANES), F32),
        vm((s.group, 16, s.px), BF16),
        vm((s.group, 2, s.width // 2, LANES), BF16),
        vm((s.group, 2, s.width // 2, LANES), BF16),
        vm((s.group, s.half, s.px), F32),
        vm((s.group, s.half, s.px), F32),
        vm((s.group, 2 * s.dp, 8, s.half), F32),
        vm((2, 2, 8, s.half), F32),
        vm((16, s.half), F32),
        vm((8, s.half), F32),
        vm((1, s.half), F32),
        vm((2, s.half, LANES), F32),
        vm((s.half, s.px), BF16),
        vm((TAPS, s.width, s.half), F32),
        vm((TAPS, s.mp, s.ch, s.half), BF16),
        vm((s.dp, TAPS, s.mp, s.rows, s.half), BF16),
        vm((s.chips, TAPS, 2, s.rows, s.half), BF16),
        vm((s.chips, TAPS, 2, s.rows, s.half), BF16),
        vm((2, TAPS, s.rows, s.half), BF16),
        vm((TAPS, s.ch, s.width), BF16),
        vm((16, s.half), F32),
        vm((2 * s.dp, 16, s.half), F32),
        vm((2, 16, s.half), F32),
        vm((s.chips, 2, 16, s.half), F32),
        vm((s.mp, 8, LANES), F32),
        dma((3,)),
        dma((1 + 2 * bits + 2 * s.chips,)),
        dma((s.mp,)),
        dma((s.dp, s.mp)),
        dma((s.dp, s.mp)),
        dma((s.mp,)),
        dma((s.mp,)),
        dma((s.group, s.chips)),
        dma((s.group, s.mp)),
        dma((s.group,)),
        dma((s.group, s.chips)),
        dma((s.group, 2)),
        dma((s.group, 2)),
        dma((s.group, near)),
        dma((s.group, 2 * s.dp)),
        dma((s.dp, TAPS)),
        dma((s.dp, TAPS)),
        dma((s.chips, groups)),
        dma((s.chips, groups)),
        dma((near, groups)),
        dma((2 * s.dp, groups)),
        dma((near,)),
        dma((2 * s.dp,)),
        dma((s.chips,)),
        dma((s.chips,)),
        dma((s.mp,)),
        dma((s.mp,)),
    ]
    flops = 2 * 2 * s.group * s.px * s.half * s.width * TAPS
    return pl.pallas_call(
        functools.partial(kernel, s),
        out_shape=(
            jax.ShapeDtypeStruct((TAPS, s.ch, s.width), BF16),
            jax.ShapeDtypeStruct((2, 16, s.half), F32),
            jax.ShapeDtypeStruct((8, LANES), F32),
        ),
        in_specs=[
            pl.BlockSpec(memory_space=pl.ANY),
            pl.BlockSpec(memory_space=pltpu.VMEM),
            pl.BlockSpec(memory_space=pl.ANY),
            pl.BlockSpec(memory_space=pltpu.VMEM),
            pl.BlockSpec(memory_space=pl.ANY),
            pl.BlockSpec(memory_space=pltpu.SMEM),
        ],
        out_specs=[pl.BlockSpec(memory_space=pltpu.VMEM)] * 3,
        scratch_shapes=scratch,
        compiler_params=pltpu.CompilerParams(
            collective_id=0, has_side_effects=True, vmem_limit_bytes=62 * 2**20
        ),
        cost_estimate=pl.CostEstimate(flops=flops, bytes_accessed=2**23, transcendentals=2**20),
        name="synthesis_step",
    )(feat, styles, weight, pack, aux, mean)


def adam_update(weight, moment, second, gradient, factor):
    clipped = gradient * factor
    moment_new = BETA_FIRST * moment + (1.0 - BETA_FIRST) * clipped
    second_new = BETA_SECOND * second + (1.0 - BETA_SECOND) * clipped * clipped
    moment_hat = moment_new / (1.0 - BETA_FIRST**STEP)
    second_hat = second_new / (1.0 - BETA_SECOND**STEP)
    weight_new = weight - LEARN_RATE * (
        moment_hat / (jnp.sqrt(second_hat) + ADAM_EPSILON) + DECAY_RATE * weight
    )
    return (moment_new, second_new, weight_new)


def block_order(x, s):
    lead = x.shape[:-1]
    x = x.reshape(lead + (2, s.px // (2 * SIDE), SIDE))
    return jnp.swapaxes(x, -3, -2).reshape(lead + (s.px,))


def local(
    mesh_shape,
    features,
    styles,
    noise_field,
    noise_keep,
    path_noise,
    length_mean,
    conv_weight,
    conv_moment,
    conv_second,
    chan_params,
    chan_moment,
    chan_second,
    rgb_weight,
    rgb_moment,
    rgb_second,
):
    s = Sizes(mesh_shape, features.shape, conv_weight.shape)
    m = lax.axis_index("mp")
    rgb_eff = rgb_weight.astype(BF16).astype(F32) * (1.0 / math.sqrt(s.width))
    noise = (noise_field.astype(F32) * noise_keep.astype(F32)).astype(BF16)
    aux = jnp.zeros((s.images, 16, s.px), BF16)
    path = block_order(jnp.swapaxes(path_noise, 0, 1), s)
    blank = functools.partial(jnp.zeros, dtype=BF16)
    aux = jnp.concatenate(
        [
            path,
            block_order(noise, s)[:, None],
            blank((s.images, 4, s.px)),
            path,
            blank((s.images, 5, s.px)),
        ],
        axis=1,
    )
    pack = jnp.concatenate(
        [
            styles.reshape(s.chips, s.group, s.ch),
            jnp.broadcast_to(chan_params[None], (s.chips, 2, s.ch)),
            jnp.zeros((s.chips, 8 - s.group - 2, s.ch), F32),
            jnp.broadcast_to(rgb_eff[None], (s.chips, 3, s.ch)),
            jnp.zeros((s.chips, 5, s.ch), F32),
        ],
        axis=1,
    )
    pack = jnp.pad(pack, ((0, 0), (0, 0), (0, LANES - s.ch)))
    wide_styles = jnp.broadcast_to(styles.T[:, :, None], (s.ch, s.images, LANES))
    taps_first = functools.partial(jnp.transpose, axes=(1, 0, 2))
    grad, sums, norm = run_kernel(
        s, features, wide_styles, taps_first(conv_weight), pack, aux, length_mean
    )
    grad_norm = norm[0, 0]
    factor = jnp.minimum(1.0, CLIP_LIMIT / (grad_norm + 1e-06))
    sums = jnp.swapaxes(sums, 0, 1).reshape(16, s.width)
    own = lax.dynamic_slice_in_dim(sums, m * s.ch, s.ch, 1)
    conv_m, conv_v, conv_new = adam_update(
        taps_first(conv_weight), taps_first(conv_moment), taps_first(conv_second), grad.astype(F32), factor
    )
    chan_m, chan_v, chan_new = adam_update(chan_params, chan_moment, chan_second, own[0:2], factor)
    rgb_m, rgb_v, rgb_new = adam_update(rgb_weight, rgb_moment, rgb_second, own[8:11], factor)
    return (
        sums[2, 0].reshape(1),
        grad_norm.reshape(1),
        taps_first(conv_m),
        taps_first(conv_v),
        taps_first(conv_new),
        taps_first(conv_new.astype(BF16)),
        chan_m,
        chan_v,
        chan_new,
        rgb_m,
        rgb_v,
        rgb_new,
        rgb_new.astype(BF16),
    )


def solution(mesh):
    whole, line = P(), P("mp", None, None)
    row, pixels = P(None, "mp"), P(None, "dp")
    in_specs = (
        P("mp", None, "dp"),
        row,
        pixels,
        pixels,
        P(None, None, "dp"),
        whole,
        line,
        line,
        line,
    ) + (row,) * 6
    out_specs = (whole, whole) + (line,) * 4 + (row,) * 7
    return jax.shard_map(
        functools.partial(local, dict(mesh.shape)),
        mesh=mesh,
        in_specs=in_specs,
        out_specs=out_specs,
        check_vma=False,
    )
```

time: 789 us -> 157 us (0.20)
  waiting for transfers between devices: 483 us -> 0 us
  Pallas kernels: 0 us -> 137 us
  blocking collectives: 99.8 us -> 0 us
  matrix products: 99.1 us -> 0 us
  other arithmetic: 38.8 us -> 7.61 us
  local copies, waits for them, and re-layouts: 40.5 us -> 9.92 us
  between operations: 18.7 us -> 2.09 us
    reduce_scatter x1 -> x0, waiting for transfers between devices: 296 us -> none  [front(): lax.psum_scatter(jnp.einsum('iko,kinp->onp', weight_low, kept_input, pref...]
    pallas_call x0 -> x1, Pallas kernels: none -> 137 us  [run_kernel(): pl.pallas_call(functools.partial(kernel, s), out_shape=(jax.ShapeDtypeStr...]
    all_gather x1 -> x0, waiting for transfers between devices: 133 us -> none  [local(): lax.all_gather(conv_grad.astype(jnp.bfloat16), 'mp', axis=0, tiled=True)]
    dot_general x6 -> x0, matrix products: 99.1 us -> none  [the longest x1 61.9 us: local(): jnp.einsum('kinp,onp->iko', kept_input, grad_piece, preferred_element_typ...]
    psum x5 -> x0, blocking collectives: 85.8 us -> none  [the longest x1 29.2 us: front(): demod_all = lax.psum(demod_part, 'mp')]
    psum x1 -> x0, waiting for transfers between devices: 41.3 us -> none  [local(): weight_grad, chan_grad = lax.psum((weight_part, chan_term), 'dp')]
    dot_general x1 -> x0, local copies, waits for them, and re-layouts: 33.1 us -> none  [front(): jnp.einsum('iko,kinp->onp', weight_low, kept_input, preferred_element_typ...]
    unnamed x10 -> x0, other arithmetic: 23.2 us -> none
  transfers between devices with their start and end apart: 5 -> 0, of which waited for: 5 -> 0; matrix products, arithmetic and copies ran while one was open for 0% -> 0% of each run, Pallas kernels for 0% -> 0%
where the time goes in v1:
time: 157 us
  Pallas kernels  137 us (87%)
  local copies, waits for them, and re-layouts  9.92 us (6%)
  other arithmetic  7.61 us (5%)
  between operations  2.09 us (1%)
    pallas_call x1, Pallas kernels, run_kernel(): pl.pallas_call(functools.partial(kernel, s), out_shape=(jax.ShapeDtypeStr...  137 us
    transpose x1, other arithmetic, local(): taps_first(conv_new.astype(BF16))  4.73 us

profile of v1, /device:TPU:0, one launch (start us, length us, event | category | flops | bytes accessed | tf_op | source)
XLA Modules:
  0.0 156.6 jit_solution(16575454953701841983)
XLA Ops:
  1.3 0.7 convert_multiply_fusion.1
  2.0 0.7 broadcast_in_dim.15
  2.7 0.7 concatenate.6
  3.4 0.6 pad.4.pack
  4.0 0.9 multiply_convert_fusion
  4.9 0.1 reshape.53
  5.0 0.1 copy.42
  5.1 0.1 broadcast_in_dim_reshape.4
  5.2 0.8 copy.31
  5.9 1.1 reshape.51
  7.0 0.2 copy.41
  7.2 0.2 reshape.52
  7.4 0.1 copy.34
  7.5 1.8 %concatenate.7.aux_hbm = bf16[16,16,1024]{2,1,0:T(8,128)(2,1)} concatenate(bf16[16,3,1024]{2,1,0:T(4,128)(2,1)S(1)} %copy.34, bf16[16,1,1024]{2,1,0:T(2,128)(2,1)S(1)} %broadcast_in_dim_reshape.4, bf16[16,4,1024]{2,1,0:T(4,128)(2,1)S(1)} %broadcast_in_dim.35, bf16[16,3,1024]{2,1,0:T(4,128)(2,1)S(1)} %copy.34, bf16[16,5,1024]{2,1,0:T(8,128)(2,1)S(1)} %broadcast_in_dim.36), dimensions={1} | concatenate | bytes 1048576 | tf_op jit(solution)/shard_map/concatenate | solution.py:869
  9.3 1.0 broadcast_in_dim.14.styles
  10.3 0.0 copy-start.2
  10.3 0.0 copy-start.5
  10.3 0.0 copy-start.6
  10.3 0.0 copy-start.1
  10.3 0.0 copy-start.3
  10.3 0.0 copy-start.4
  10.3 0.0 copy-start
  10.4 136.9 %synthesis_step.1 = (bf16[9,64,512]{2,1,0:T(8,128)(2,1)}, f32[2,16,256]{2,1,0:T(8,128)}, f32[8,128]{1,0:T(8,128)}) custom-call(bf16[64,16,1024]{2,1,0:T(8,128)(2,1)} %feat_hbm.1, f32[64,16,128]{2,1,0:T(8,128)} %broadcast_in_dim.14.styles, f32[9,64,512]{2,1,0:T(8,128)} %bitcast.43, f32[4,16,128]{2,1,0:T(8,128)} %pad.4.pack, ...), custom_call_target="tpu_custom_call" | custom-call | flops 19327352832 | bytes 8388608 | tf_op jit(solution)/shard_map/synthesis_step/pallas_call | solution.py:801
  147.3 1.2 slice.13
  149.2 0.8 copy.38
  150.0 0.5 slice.16
  150.5 0.0 copy-done.2
  150.5 0.0 copy-done.5
  150.5 0.0 copy-done.6
  150.5 0.7 multiply_subtract_fusion.2
  151.1 0.0 copy-done.1
  151.1 0.0 copy-done.3
  151.1 0.0 copy-done.4
  151.2 0.7 fusion.5
  151.8 0.0 copy-done
  151.8 4.7 %convert_bitcast_fusion = (bf16[64,9,512]{2,0,1:T(8,128)(2,1)}, f32[9,64,512]{2,1,0:T(8,128)}, f32[64,9,512]{2,0,1:T(8,128)}, f32[64,9,512]{2,0,1:T(8,128)}) fusion(f32[64,9,512]{2,0,1:T(8,128)} %param.23, f32[]{:T(128)} %bitcast.10, bf16[9,64,512]{2,1,0:T(8,128)(2,1)} %get-tuple-element.18, f32[64,9,512]{2,0,1:T(8,128)} %param.22, f32[64,9,512]{2,0,1:T(8,128)S(1)} %copy-done), kind=kLoop, calls=%fused_computation.6 | loop fusion | flops 5013504 | bytes 8257540 | tf_op jit(solution)/shard_map/transpose | solution.py:910
  (5 shorter events, 0.1 us)
Async XLA Ops:
  10.3 140.2 %copy-start.2 = (f32[2,64]{1,0:T(2,128)S(1)}, f32[2,64]{1,0:T(2,128)}, u32[]{:S(2)}) copy-start(f32[2,64]{1,0:T(2,128)} %param.24) | copy-start | bytes 1540
  10.3 140.2 %copy-start.5 = (f32[2,64]{1,0:T(2,128)S(1)}, f32[2,64]{1,0:T(2,128)}, u32[]{:S(2)}) copy-start(f32[2,64]{1,0:T(2,128)} %param.26) | copy-start | bytes 1540
  10.3 140.2 %copy-start.6 = (f32[2,64]{1,0:T(2,128)S(1)}, f32[2,64]{1,0:T(2,128)}, u32[]{:S(2)}) copy-start(f32[2,64]{1,0:T(2,128)} %param.25) | copy-start | bytes 1540
  10.3 140.8 %copy-start.1 = (f32[3,64]{1,0:T(4,128)S(1)}, f32[3,64]{1,0:T(4,128)}, u32[]{:S(2)}) copy-start(f32[3,64]{1,0:T(4,128)} %param.27) | copy-start | bytes 2308
  10.3 140.8 %copy-start.3 = (f32[3,64]{1,0:T(4,128)S(1)}, f32[3,64]{1,0:T(4,128)}, u32[]{:S(2)}) copy-start(f32[3,64]{1,0:T(4,128)} %param.29) | copy-start | bytes 2308
  10.3 140.8 %copy-start.4 = (f32[3,64]{1,0:T(4,128)S(1)}, f32[3,64]{1,0:T(4,128)}, u32[]{:S(2)}) copy-start(f32[3,64]{1,0:T(4,128)} %param.28) | copy-start | bytes 2308
  10.3 141.5 %copy-start = (f32[64,9,512]{2,0,1:T(8,128)S(1)}, f32[64,9,512]{2,0,1:T(8,128)}, u32[]{:S(2)}) copy-start(f32[64,9,512]{2,0,1:T(8,128)} %param.21) | copy-start | bytes 3538948

commit v2 on v1

v2 whole, which is shorter than its diff:
```python
import functools
import math

import jax
import jax.numpy as jnp
from jax import lax
from jax.experimental import pallas as pl
from jax.experimental.pallas import tpu as pltpu
from jax.sharding import PartitionSpec as P

SIDE = 64
STEP = 5
TAPS = 9
LANES = 128

CLIP_LIMIT = 0.1
LEARN_RATE = 0.3
DECAY_RATE = 0.01
BETA_FIRST = 0.5
BETA_SECOND = 0.5
ADAM_EPSILON = 1e-08
DEMOD_EPSILON = 1e-08
HIGHEST = lax.Precision.HIGHEST
MESH = pl.DeviceIdType.MESH
F32 = jnp.float32
BF16 = jnp.bfloat16
NT = (((1,), (1,)), ((), ()))


class Sizes:
    def __init__(self, mesh_shape, features, conv_weight):
        self.dp = mesh_shape["dp"]
        self.mp = mesh_shape["mp"]
        self.chips = self.mp // 2
        self.ch, self.images, self.px = features
        self.width = conv_weight[2]
        self.half = self.width // 2
        self.group = self.images // self.chips
        self.blocks = self.px // LANES
        self.ext = self.px + 2 * LANES
        self.split = (self.ch // self.dp) % 16 == 0
        self.shares = self.dp if self.split else 1
        self.rows = self.ch // self.shares
        self.taps_each = 3
        self.first = 6
        self.bits = []
        bit = self.chips // 2
        while bit >= 1:
            self.bits.append(bit)
            bit //= 2


def flip(value, bit):
    return value + bit - 2 * bit * lax.rem(lax.div(value, bit), 2)


def swap_halves(x):
    return pltpu.roll(x, SIDE, x.ndim - 1)


def kernel(
    s,
    feat_hbm,
    styles,
    weight_hbm,
    chan,
    rgb,
    path_hbm,
    field_hbm,
    keep_hbm,
    mean,
    grad_out,
    small_out,
    norm_out,
    feat,
    style_cols,
    turned,
    outbox,
    grids,
    weight_own,
    weight_low,
    weights,
    weights_t,
    weight_sq,
    pack,
    pack_all,
    columns,
    rgb_low,
    rgb_rows,
    demod_rows,
    demod_cols,
    chan_cols,
    path,
    field,
    keep,
    pixel_rows,
    aux_rows,
    aux,
    halo_out,
    halo_in,
    scaled,
    slope_of,
    proj_all,
    half_pick,
    stat_rows,
    rgb_acc,
    loss_acc,
    chan_acc,
    grad_conv,
    total,
    share_out,
    share_in,
    line_out,
    line_in,
    wide_out,
    wide_in,
    wide_sum,
    narrow_in,
    final,
    gathered,
    small_own,
    small_plane,
    small_mid,
    small_line,
    small_sum,
    square_all,
    in_sem,
    w_send,
    w_recv,
    p_sem,
    f_send,
    f_recv,
    f_local,
    h_send,
    h_recv,
    j_send,
    j_recv,
    r_send,
    r_recv,
    l_send,
    l_recv,
    b_recv,
    n_recv,
    g_sem,
    sp_sem,
    sl_sem,
    n_sem,
):
    d = lax.axis_index("dp")
    m = lax.axis_index("mp")
    z = lax.div(m, 2)
    c = lax.rem(m, 2)
    other = 1 - c
    mate = 2 * z + other
    conv_gain = 1.0 / math.sqrt(TAPS * s.width)
    rgb_gain = 1.0 / math.sqrt(s.width)
    last = s.group - 1

    def copy_to(src, dst, send, recv, dd, mm):
        return pltpu.make_async_remote_copy(
            src_ref=src, dst_ref=dst, send_sem=send, recv_sem=recv, device_id=(dd, mm), device_id_type=MESH
        )

    def taken(ref, sem):
        copy_to(ref, ref, sem, sem, d, mate).wait_recv()

    def gone(ref, sem):
        copy_to(ref, ref, sem, sem, d, mate).wait_send()

    def z_at(r):
        return lax.rem(z + r, s.chips)

    def d_at(r):
        return lax.rem(d + r, s.dp)

    line = [(d, lax.rem(m + r, s.mp)) for r in range(1, s.mp)]
    plane = [(d_at(r), mm) for r in range(1, s.dp) for mm in (m, mate)]
    near = plane + [(d, mate)]
    place = 2 * d + c

    get_weight = pltpu.make_async_copy(weight_hbm, weight_own, in_sem.at[0])
    get_feat = pltpu.make_async_copy(feat_hbm, feat, in_sem.at[1])
    get_path = pltpu.make_async_copy(path_hbm, path, in_sem.at[2])
    get_field = pltpu.make_async_copy(field_hbm, field, in_sem.at[3])
    get_keep = pltpu.make_async_copy(keep_hbm, keep, in_sem.at[4])
    get_weight.start()
    get_feat.start()
    get_path.start()
    get_field.start()
    get_keep.start()
    halo_in[...] = jnp.zeros_like(halo_in)
    barrier = pltpu.get_barrier_semaphore()
    for dd, mm in line + plane:
        pl.semaphore_signal(barrier, inc=1, device_id=(dd, mm), device_id_type=MESH)
    pack[...] = jnp.zeros_like(pack)
    rgb_low[...] = rgb[...].astype(BF16)
    rgb_eff = rgb_low[...].astype(F32) * rgb_gain
    for zz in range(s.chips):
        pack[zz, : s.group, : s.ch] = styles[zz * s.group : (zz + 1) * s.group, :]
        pack[zz, s.group : s.group + 2, : s.ch] = chan[...]
        pack[zz, 8:11, : s.ch] = rgb_eff
    pack_all[m] = pack[z]
    for i in range(s.ch):
        style_cols[i] = jnp.broadcast_to(styles[:, i : i + 1], (s.images, LANES))

    get_weight.wait()
    for k in range(TAPS):
        weight_low[k] = weight_own[k].astype(BF16)
    pl.semaphore_wait(barrier, len(line) + len(plane))

    share = d if s.split else 0

    def piece(m_of):
        return weights.at[:, pl.ds(pl.multiple_of(m_of * s.ch + share * s.rows, 16), s.rows), :]

    def own_piece(half_of):
        return weight_low.at[
            :,
            pl.ds(pl.multiple_of(share * s.rows, 16), s.rows),
            pl.ds(pl.multiple_of(half_of * s.half, LANES), s.half),
        ]

    sent_rows = 0
    for index, bit in enumerate(s.bits):
        for cc in range(2):
            copy_to(
                own_piece(cc), piece(m), w_send.at[0], w_recv.at[index], d, 2 * flip(z, bit) + cc
            ).start()
            sent_rows += s.rows
    copy_to(
        weight_low.at[:, :, pl.ds(pl.multiple_of(other * s.half, LANES), s.half)],
        weights.at[:, pl.ds(pl.multiple_of(m * s.ch, 16), s.ch), :],
        w_send.at[0],
        w_recv.at[len(s.bits)],
        d,
        mate,
    ).start()
    sent_rows += s.ch
    for dd, mm in line:
        copy_to(pack.at[lax.div(mm, 2)], pack_all.at[m], p_sem.at[0], p_sem.at[1], dd, mm).start()

    get_feat.wait()
    lane = lax.broadcasted_iota(jnp.int32, (1, 1, LANES), 2)
    low_lanes = lane < SIDE
    step = 8

    def modulate(index, carry):
        rows = pl.ds(pl.multiple_of(index * step, step), step)
        factor = style_cols[rows]
        for q in range(s.blocks // 2):
            first = feat[rows, :, q * LANES : (q + 1) * LANES].astype(F32) * factor
            q2 = q + s.blocks // 2
            second = feat[rows, :, q2 * LANES : (q2 + 1) * LANES].astype(F32) * factor
            even = jnp.where(low_lanes, first, swap_halves(second))
            odd = jnp.where(low_lanes, swap_halves(first), second)
            out_rows = pl.ds(pl.multiple_of(index * step * s.images, step * 8), step * s.images)
            turned[2 * q, out_rows, :] = even.reshape(step * s.images, LANES)
            turned[2 * q + 1, out_rows, :] = odd.reshape(step * s.images, LANES)
        return carry

    lax.fori_loop(0, s.ch // step, modulate, 0)

    def pick(n, carry):
        for j in range(s.blocks):
            part = turned[j, pl.ds(n, s.ch, stride=s.images), :]
            outbox[n, :, j * LANES : (j + 1) * LANES] = part.astype(BF16)
        return carry

    lax.fori_loop(0, s.images, pick, 0)

    middle = pl.ds(LANES, s.px)

    def grid_rows(m_of):
        return pl.ds(pl.multiple_of(m_of * s.ch, 16), s.ch)

    def feature_send(q, r):
        zz = z_at(r)
        return copy_to(
            outbox.at[zz * s.group + q],
            grids.at[q, 1, grid_rows(m), middle],
            f_send.at[q],
            f_recv.at[q, 0],
            d,
            2 * zz + c,
        )

    def start_features():
        for q in range(s.group):
            own = outbox.at[z * s.group + q]
            there = grids.at[q, 1, grid_rows(m), middle]
            pltpu.make_async_copy(own, there, f_local.at[0]).start()
            copy_to(own, there, f_send.at[q], f_recv.at[q, 1], d, mate).start()
            if q < 2:
                for r in range(1, s.chips):
                    feature_send(q, r).start()

    held = [z]
    plane_rows = 0
    for index, bit in enumerate(s.bits):
        peer = flip(z, bit)
        for h in held[1:]:
            for cc in range(2):
                at = piece(2 * h + cc)
                copy_to(at, at, w_send.at[0], w_recv.at[index], d, 2 * peer + c).start()
                sent_rows += s.rows
        if index == len(s.bits) - 1:
            start_features()
        fresh = [flip(h, bit) for h in held]
        taken(weights.at[:, pl.ds(0, 2 * len(fresh) * s.rows), :], w_recv.at[index])
        if s.split:
            for h in fresh:
                for cc in range(2):
                    at = piece(2 * h + cc)
                    for r in range(1, s.dp):
                        copy_to(at, at, w_send.at[1], w_recv.at[len(s.bits) + 1], d_at(r), m).start()
                        plane_rows += s.rows
        held = held + fresh

    weights[:, grid_rows(m), :] = weight_low[:, :, pl.ds(pl.multiple_of(c * s.half, LANES), s.half)]
    get_path.wait()
    get_field.wait()
    get_keep.wait()
    lane2 = lax.broadcasted_iota(jnp.int32, (1, LANES), 1)
    low2 = lane2 < SIDE
    for k in range(4):
        for q in range(s.blocks // 2):
            q2 = q + s.blocks // 2
            cuts = [slice(q * LANES, (q + 1) * LANES), slice(q2 * LANES, (q2 + 1) * LANES)]
            if k < 3:
                first, second = [path[k, :, cut].astype(F32) for cut in cuts]
            else:
                first, second = [field[:, cut].astype(F32) * keep[:, cut].astype(F32) for cut in cuts]
            pixel_rows[k, :, 2 * q * LANES : (2 * q + 1) * LANES] = jnp.where(low2, first, swap_halves(second))
            pixel_rows[k, :, (2 * q + 1) * LANES : (2 * q + 2) * LANES] = jnp.where(low2, swap_halves(first), second)
    aux_rows[...] = jnp.zeros_like(aux_rows)
    for q in range(s.group):
        for k in range(4):
            row = pixel_rows[k, pl.ds(z * s.group + q, 1), :]
            aux_rows[q, k : k + 1, :] = row
            if k < 3:
                aux_rows[q, 8 + k : 9 + k, :] = row
        aux[q] = aux_rows[q].astype(BF16)

    taken(pack_all.at[pl.ds(0, s.mp - 1)], p_sem.at[1])
    for mm in range(s.mp):
        columns[mm * s.ch : (mm + 1) * s.ch, :] = pack_all[mm].T[: s.ch, :]
    rows_all = columns[...].T
    for h in range(2):
        rgb_rows[h] = rows_all[8:16, h * s.half : (h + 1) * s.half]
    mine = columns[pl.ds(pl.multiple_of(c * s.half, 8), s.half), :]
    for k in range(2):
        chan_cols[k] = jnp.broadcast_to(mine[:, s.group + k : s.group + k + 1], (s.half, LANES))
    total[...] = jnp.zeros_like(total)
    stat_rows[...] = jnp.zeros_like(stat_rows)
    rgb_acc[...] = jnp.zeros_like(rgb_acc)
    loss_acc[...] = jnp.zeros_like(loss_acc)
    chan_acc[...] = jnp.zeros_like(chan_acc)

    column = lax.rem(lane2, SIDE)
    not_first = column >= 1
    not_last = column <= SIDE - 2
    pair = s.width // 2
    up = lax.rem(d + s.dp - 1, s.dp)
    down = lax.rem(d + 1, s.dp)

    def halo_up(q):
        return copy_to(halo_out.at[q, 0], halo_in.at[q, 1], h_send.at[q, 0], h_recv.at[q, 1], up, m)

    def halo_down(q):
        return copy_to(halo_out.at[q, 1], halo_in.at[q, 0], h_send.at[q, 1], h_recv.at[q, 0], down, m)

    def ends(q):
        return grids[q, 1, :, LANES : 2 * LANES], grids[q, 1, :, s.px : s.px + LANES]

    def take_line(q):
        taken(grids.at[q, 1, pl.ds(0, (s.chips - 1) * s.ch), middle], f_recv.at[q, 0])
        for r in range(1, s.chips):
            at = grids.at[q, 1, grid_rows(2 * z_at(r) + c), middle]
            copy_to(at, at, f_send.at[q], f_recv.at[q, 1], d, mate).start()

        @pl.when(q + 2 < s.group)
        def _():
            for r in range(1, s.chips):
                feature_send(q + 2, r).start()

    def take_mate(q):
        taken(grids.at[q, 1, pl.ds(0, s.chips * s.ch), middle], f_recv.at[q, 1])
        top, end = ends(q)
        halo_out[q, 0] = jnp.where(low2, top[:pair], swap_halves(top[pair:]))
        halo_out[q, 1] = jnp.where(low2, swap_halves(end[:pair]), end[pair:])

        @pl.when(d > 0)
        def _():
            halo_up(q).start()

        @pl.when(d < s.dp - 1)
        def _():
            halo_down(q).start()

    def lateral(q, j):
        x = grids[q, 1, :, j * LANES : (j + 1) * LANES]
        none = jnp.zeros_like(x)
        grids[q, 0, :, j * LANES : (j + 1) * LANES] = jnp.where(not_first, pltpu.roll(x, 1, 1), none)
        grids[q, 2, :, j * LANES : (j + 1) * LANES] = jnp.where(not_last, pltpu.roll(x, LANES - 1, 1), none)

    def inner(q):
        for j in range(1, s.blocks + 1):
            lateral(q, j)

    def border(q):
        @pl.when(d > 0)
        def _():
            halo_down(q).wait_recv()

        @pl.when(d < s.dp - 1)
        def _():
            halo_up(q).wait_recv()

        top, end = ends(q)
        above = halo_in[q, 0]
        below = halo_in[q, 1]
        swapped_end = swap_halves(end)
        swapped_top = swap_halves(top)
        grids[q, 1, :pair, :LANES] = jnp.where(low2, above, swapped_end[:pair])
        grids[q, 1, pair:, :LANES] = jnp.where(low2, swap_halves(above), swapped_end[pair:])
        tail = s.px + LANES
        grids[q, 1, :pair, tail : tail + LANES] = jnp.where(low2, swapped_top[:pair], swap_halves(below))
        grids[q, 1, pair:, tail : tail + LANES] = jnp.where(low2, swapped_top[pair:], below)
        lateral(q, 0)
        lateral(q, s.blocks + 1)

    def convolve_math(q):
        projected = jnp.zeros((16, s.half), F32)
        wide = 2 * LANES
        for p in range(0, s.px, wide):
            acc = jnp.zeros((s.half, wide), F32)
            for a in range(3):
                for b in range(3):
                    k = 3 * a + b
                    acc += jnp.dot(
                        weights_t[:, k * s.width : (k + 1) * s.width],
                        grids[q, b, :, a * LANES + p : a * LANES + p + wide],
                        preferred_element_type=F32,
                    )
            acts = []
            for t in range(2):
                cut = slice(p + t * LANES, p + (t + 1) * LANES)
                conv = acc[:, t * LANES : (t + 1) * LANES] * conv_gain
                noise = aux[q, :, cut].astype(F32)[3:4]
                pre = conv * demod_cols[q] + chan_cols[1] * noise + chan_cols[0]
                sig = jax.nn.sigmoid(pre)
                act = pre * sig
                scaled[q, :, cut] = conv
                slope_of[q, :, cut] = sig * (1.0 + pre * (1.0 - sig))
                acts.append(act.astype(BF16))
            act = jnp.concatenate(acts, axis=1)
            projected += lax.dot_general(aux[q, :, p : p + wide], act, NT, preferred_element_type=F32)
        proj_all[q, place] = projected[:8]

    def convolve(q):
        convolve_math(q)
        for dd, mm in near:
            at = proj_all.at[q, place]
            copy_to(at, at, j_send.at[q], j_recv.at[q], dd, mm).start()

    def signal_back(q):
        taken(proj_all.at[q, pl.ds(0, 2 * s.dp - 1)], j_recv.at[q])
        signal_math(q)

    def signal_math(q):
        halves = []
        for h in range(2):
            acc = proj_all[q, h]
            for dd in range(1, s.dp):
                acc = acc + proj_all[q, 2 * dd + h]
            halves.append(acc)
        slopes = [jnp.sum(rgb_rows[h] * halves[h], axis=0, keepdims=True) for h in range(2)]
        row = lax.broadcasted_iota(jnp.int32, (8, s.half), 0)
        length_sq = jnp.sum(slopes[0] * slopes[0] + slopes[1] * slopes[1], axis=1, keepdims=True)
        length = jnp.sqrt(length_sq + 1e-08)
        excess = length - mean[0]
        loss_acc[...] += jnp.broadcast_to(excess * excess, (1, s.half))
        scale = 2.0 * excess / length
        for h in range(2):
            grad = scale * slopes[h]
            half_pick[h, 0] = grad * rgb_rows[h]
            half_pick[h, 1] = jnp.where(row < 3, grad * halves[h] * rgb_gain, 0.0)
        rgb_acc[...] += half_pick[c, 1]
        coef = half_pick[c, 0]
        high = coef.astype(BF16).astype(F32)
        coef_t = jnp.concatenate([high, coef - high], axis=0).T.astype(BF16)
        wide = 2 * LANES
        bias_part = chan_acc[0]
        strength_part = chan_acc[1]
        stat_part = jnp.zeros((s.half, LANES), F32)
        back = demod_cols[q] * conv_gain
        for p in range(0, s.px, wide):
            act_grad = jnp.dot(coef_t, aux[q, :, p : p + wide], preferred_element_type=F32)
            for t in range(2):
                cut = slice(p + t * LANES, p + (t + 1) * LANES)
                noise = aux[q, :, cut].astype(F32)[3:4]
                grad = act_grad[:, t * LANES : (t + 1) * LANES] * slope_of[q, :, cut]
                bias_part = bias_part + grad
                strength_part = strength_part + grad * noise
                stat_part = stat_part + grad * scaled[q, :, cut]
                grad_conv[lax.rem(q, 2), :, cut] = (grad * back).astype(BF16)
        chan_acc[0] = bias_part
        chan_acc[1] = strength_part
        stat = jnp.sum(stat_part.T, axis=0, keepdims=True)
        dem = demod_rows[pl.ds(q, 1), :]
        stat_rows[pl.ds(q, 1), :] = stat * (dem * dem * dem) * (-0.5 * conv_gain * conv_gain)

    def tap_grad(q, k):
        a, b = k // 3, k % 3
        return lax.dot_general(
            grids[q, b, :, a * LANES : a * LANES + s.px], grad_conv[lax.rem(q, 2)], NT, preferred_element_type=F32
        )

    pltpu.make_async_copy(
        grids.at[0, 1, pl.ds(0, s.group * s.ch), middle],
        grids.at[0, 1, pl.ds(0, s.group * s.ch), middle],
        f_local.at[0],
    ).wait()
    take_line(0)
    take_mate(0)
    inner(0)
    border(0)

    taken(weights.at[:, pl.ds(0, s.ch), :], w_recv.at[len(s.bits)])
    if s.split:
        taken(weights.at[:, pl.ds(0, plane_rows), :], w_recv.at[len(s.bits) + 1])
    square = jnp.zeros((s.width, s.half), F32)
    for k in range(TAPS):
        w = weights[k]
        weights_t[:, k * s.width : (k + 1) * s.width] = w.T
        wf = w.astype(F32)
        square = square + wf * wf
    weight_sq[...] = square
    demod_sq = jnp.dot(rows_all * rows_all, weight_sq[...], precision=HIGHEST, preferred_element_type=F32)
    demod = lax.rsqrt(conv_gain * conv_gain * demod_sq + DEMOD_EPSILON)
    demod_rows[...] = demod
    demod_t = demod.T
    for q in range(s.group):
        demod_cols[q] = jnp.broadcast_to(demod_t[:, q : q + 1], (s.half, LANES))

    def add_taps(q, taps):
        for k in taps:
            total[k] += tap_grad(q, k)

    def stage(q, carry):
        convolve(q)
        take_line(q + 1)

        @pl.when(q > 0)
        def _():
            add_taps(q - 1, range(TAPS // 2))

        take_mate(q + 1)

        @pl.when(q > 0)
        def _():
            add_taps(q - 1, range(TAPS // 2, TAPS))

        signal_back(q)
        inner(q + 1)
        border(q + 1)
        return carry

    lax.fori_loop(0, last, stage, 0)

    convolve(last)
    add_taps(last - 1, range(TAPS))
    signal_back(last)
    small_own[0:1] = jnp.sum(chan_acc[0].T, axis=0, keepdims=True)
    small_own[1:2] = jnp.sum(chan_acc[1].T, axis=0, keepdims=True)
    small_own[2:3] = loss_acc[...]
    small_own[3:8] = jnp.zeros((5, s.half), F32)
    small_own[8:16] = rgb_acc[...]
    small_plane[place] = small_own[...]
    for dd, mm in near:
        copy_to(small_own, small_plane.at[place], sp_sem.at[0], sp_sem.at[1], dd, mm).start()
    cross = 2.0 * jnp.dot(
        columns[...] * columns[...], stat_rows[...], precision=HIGHEST, preferred_element_type=F32
    )
    weight_sq[...] = cross

    def share_rows(share_of):
        return pl.ds(pl.multiple_of(share_of * s.rows, 16), s.rows)

    own_rows = share_rows(share)
    own_cols = pl.ds(pl.multiple_of(c * s.half, LANES), s.half)
    targets = near if s.split else [(d, mate)]

    def last_tap(k):
        grad = total[k] + tap_grad(last, k) + weights[k].astype(F32) * weight_sq[...]
        grad = grad.astype(BF16).reshape(s.mp, s.ch, s.half)
        if k < s.first:
            share_out[k] = grad
            for r in range(1, s.dp):
                part = share_out.at[k, :, share_rows(d_at(r) if s.split else 0), :]
                copy_to(part, share_in.at[d, k], r_send.at[0], r_recv.at[k], d_at(r), m).start()
        else:
            b = k - s.first
            wide_out[b] = grad
            for r in range(1, s.chips):
                part = wide_out.at[b, pl.ds(2 * z_at(r), 2)]
                copy_to(part, wide_in.at[r, b], l_send.at[1], b_recv.at[b], d, 2 * z_at(r) + c).start()

    def by_shares(own, parts):
        acc = None
        for dd in range(s.dp):
            term = jnp.where(d == dd, own, parts[dd].astype(F32))
            acc = term if acc is None else acc + term
        return acc

    def plane_done(k):
        taken(share_in.at[pl.ds(0, s.dp - 1), k], r_recv.at[k])
        acc = by_shares(share_out[k, :, own_rows, :].astype(F32), [share_in[dd, k] for dd in range(s.dp)])
        line_out[:, k] = acc.astype(BF16).reshape(s.chips, 2, s.rows, s.half)
        for r in range(1, s.chips):
            copy_to(
                line_out.at[z_at(r), k], line_in.at[r, k], l_send.at[0], l_recv.at[k], d, 2 * z_at(r) + c
            ).start()

    def line_done(b):
        taken(wide_in.at[pl.ds(1, s.chips - 1), b], b_recv.at[b])
        acc = wide_out[b, pl.ds(2 * z, 2)].astype(F32)
        for r in range(1, s.chips):
            acc = acc + wide_in[r, b].astype(F32)
        wide_sum[b] = acc.astype(BF16)
        for r in range(1, s.dp):
            part = wide_sum.at[b, :, share_rows(d_at(r) if s.split else 0), :]
            copy_to(part, narrow_in.at[d, b], r_send.at[1], n_recv.at[b], d_at(r), m).start()

    def byte_count():
        return weights.at[:, pl.ds(0, len(targets) * s.rows), :]

    def finish(first_tap):
        for k in range(first_tap, first_tap + s.taps_each):
            if k < s.first:
                taken(line_in.at[pl.ds(1, s.chips - 1), k], l_recv.at[k])
                acc = line_out[z, k].astype(F32)
                for r in range(1, s.chips):
                    acc = acc + line_in[r, k].astype(F32)
            else:
                b = k - s.first
                taken(narrow_in.at[pl.ds(0, s.dp - 1), b], n_recv.at[b])
                acc = by_shares(wide_sum[b, :, own_rows, :].astype(F32), [narrow_in[dd, b] for dd in range(s.dp)])
            final[:, k] = acc.astype(BF16)
            gathered[k, own_rows, own_cols] = final[c, k]
        taps = pl.ds(first_tap, s.taps_each)
        for dd, mm in targets:
            copy_to(
                final.at[lax.rem(mm, 2), taps],
                gathered.at[taps, own_rows, own_cols],
                g_sem.at[0],
                g_sem.at[1],
                dd,
                mm,
            ).start()

    for k in (0, 6, 1, 2, 7, 3, 4, 8, 5):
        last_tap(k)

    taken(small_plane.at[pl.ds(0, 2 * s.dp - 1)], sp_sem.at[1])
    for h in range(2):
        acc = small_plane[h, 0:8]
        for dd in range(1, s.dp):
            acc = acc + small_plane[2 * dd + h, 0:8]
        row = lax.broadcasted_iota(jnp.int32, (8, s.half), 0)
        small_mid[h, 0:8] = jnp.where(row < 2, acc, small_plane[h, 0:8])
        small_mid[h, 8:16] = small_plane[h, 8:16]
    small_line[z] = small_mid[...]
    for r in range(1, s.chips):
        copy_to(small_mid, small_line.at[z], sl_sem.at[0], sl_sem.at[1], d, 2 * z_at(r) + c).start()

    plane_done(0)
    line_done(0)
    plane_done(1)
    plane_done(2)
    line_done(1)
    plane_done(3)
    finish(0)
    plane_done(4)
    line_done(2)
    plane_done(5)
    finish(6)
    finish(3)
    taken(small_line.at[pl.ds(0, s.chips - 1)], sl_sem.at[1])
    sums = small_line[0]
    for zz in range(1, s.chips):
        sums = sums + small_line[zz]
    small_sum[...] = sums
    chan_squares = jnp.sum(sums[:, 0:2] * sums[:, 0:2]) + jnp.sum(sums[:, 8:16] * sums[:, 8:16])
    start = m * s.ch
    first = lax.rem(start, s.half)
    block = pl.multiple_of(lax.div(first, LANES) * LANES, LANES)
    mine = small_sum[lax.div(start, s.half), :, pl.ds(block, LANES)]
    small_out[...] = pltpu.roll(mine, lax.rem(2 * LANES - lax.rem(first, LANES), LANES), 1)

    taken(byte_count(), g_sem.at[1])
    acc = jnp.zeros((s.ch, s.width), F32)
    for k in range(TAPS):
        grad = gathered[k].astype(F32)
        acc = acc + grad * grad
    square_all[m] = jnp.broadcast_to(jnp.sum(acc, keepdims=True), (8, LANES))
    for dd, mm in line:
        copy_to(square_all.at[m], square_all.at[m], n_sem.at[0], n_sem.at[1], dd, mm).start()
    grad_out[...] = gathered[...]
    taken(square_all.at[pl.ds(0, s.mp - 1)], n_sem.at[1])
    acc = square_all[0]
    for mm in range(1, s.mp):
        acc = acc + square_all[mm]
    norm_out[...] = jnp.sqrt(acc + chan_squares)

    gone(weights.at[:, pl.ds(0, sent_rows), :], w_send.at[0])
    if s.split:
        gone(weights.at[:, pl.ds(0, plane_rows), :], w_send.at[1])
    gone(pack_all.at[pl.ds(0, s.mp - 1)], p_sem.at[0])
    for q in range(s.group):
        gone(grids.at[q, 1, pl.ds(0, (2 * s.chips - 1) * s.ch), middle], f_send.at[q])
        gone(proj_all.at[q, pl.ds(0, 2 * s.dp - 1)], j_send.at[q])
    gone(small_plane.at[pl.ds(0, 2 * s.dp - 1)], sp_sem.at[0])
    gone(share_in.at[pl.ds(0, s.dp - 1)], r_send.at[0])
    gone(small_line.at[pl.ds(0, s.chips - 1)], sl_sem.at[0])
    gone(line_in.at[pl.ds(1, s.chips - 1)], l_send.at[0])
    gone(wide_in.at[pl.ds(1, s.chips - 1)], l_send.at[1])
    gone(narrow_in.at[pl.ds(0, s.dp - 1)], r_send.at[1])
    gone(byte_count(), g_sem.at[0])
    gone(square_all.at[pl.ds(0, s.mp - 1)], n_sem.at[0])

    @pl.when(d > 0)
    def _():
        for q in range(s.group):
            halo_up(q).wait_send()

    @pl.when(d < s.dp - 1)
    def _():
        for q in range(s.group):
            halo_down(q).wait_send()


def run_kernel(s, *operands):
    vm, dma = pltpu.VMEM, pltpu.SemaphoreType.DMA
    rest = TAPS - s.first
    scratch = [
        vm((s.ch, s.images, s.px), BF16),
        vm((s.ch, s.images, LANES), F32),
        vm((s.blocks, s.ch * s.images, LANES), F32),
        vm((s.images, s.ch, s.px), BF16),
        vm((s.group, 3, s.width, s.ext), BF16),
        vm((TAPS, s.ch, s.width), F32),
        vm((TAPS, s.ch, s.width), BF16),
        vm((TAPS, s.width, s.half), BF16),
        vm((s.half, TAPS * s.width), BF16),
        vm((s.width, s.half), F32),
        vm((s.chips, 16, LANES), F32),
        vm((s.mp, 16, LANES), F32),
        vm((s.width, 16), F32),
        vm((3, s.ch), BF16),
        vm((2, 8, s.half), F32),
        vm((16, s.half), F32),
        vm((s.group, s.half, LANES), F32),
        vm((2, s.half, LANES), F32),
        vm((3, s.images, s.px), BF16),
        vm((s.images, s.px), BF16),
        vm((s.images, s.px), jnp.int32),
        vm((4, s.images, s.px), F32),
        vm((s.group, 16, s.px), F32),
        vm((s.group, 16, s.px), BF16),
        vm((s.group, 2, s.width // 2, LANES), BF16),
        vm((s.group, 2, s.width // 2, LANES), BF16),
        vm((s.group, s.half, s.px), F32),
        vm((s.group, s.half, s.px), F32),
        vm((s.group, 2 * s.dp, 8, s.half), F32),
        vm((2, 2, 8, s.half), F32),
        vm((16, s.half), F32),
        vm((8, s.half), F32),
        vm((1, s.half), F32),
        vm((2, s.half, LANES), F32),
        vm((2, s.half, s.px), BF16),
        vm((TAPS, s.width, s.half), F32),
        vm((s.first, s.mp, s.ch, s.half), BF16),
        vm((s.dp, s.first, s.mp, s.rows, s.half), BF16),
        vm((s.chips, s.first, 2, s.rows, s.half), BF16),
        vm((s.chips, s.first, 2, s.rows, s.half), BF16),
        vm((rest, s.mp, s.ch, s.half), BF16),
        vm((s.chips, rest, 2, s.ch, s.half), BF16),
        vm((rest, 2, s.ch, s.half), BF16),
        vm((s.dp, rest, 2, s.rows, s.half), BF16),
        vm((2, TAPS, s.rows, s.half), BF16),
        vm((TAPS, s.ch, s.width), BF16),
        vm((16, s.half), F32),
        vm((2 * s.dp, 16, s.half), F32),
        vm((2, 16, s.half), F32),
        vm((s.chips, 2, 16, s.half), F32),
        vm((2, 16, s.half), F32),
        vm((s.mp, 8, LANES), F32),
        dma((5,)),
        dma((2,)),
        dma((len(s.bits) + 2,)),
        dma((2,)),
        dma((s.group,)),
        dma((s.group, 2)),
        dma((1,)),
        dma((s.group, 2)),
        dma((s.group, 2)),
        dma((s.group,)),
        dma((s.group,)),
        dma((2,)),
        dma((s.first,)),
        dma((2,)),
        dma((s.first,)),
        dma((rest,)),
        dma((rest,)),
        dma((2,)),
        dma((2,)),
        dma((2,)),
        dma((2,)),
    ]
    flops = 2 * 2 * s.group * s.px * s.half * s.width * TAPS
    here, there = pl.BlockSpec(memory_space=pltpu.VMEM), pl.BlockSpec(memory_space=pl.ANY)
    return pl.pallas_call(
        functools.partial(kernel, s),
        out_shape=(
            jax.ShapeDtypeStruct((TAPS, s.ch, s.width), BF16),
            jax.ShapeDtypeStruct((16, LANES), F32),
            jax.ShapeDtypeStruct((8, LANES), F32),
        ),
        in_specs=[there, here, there, here, here, there, there, there, pl.BlockSpec(memory_space=pltpu.SMEM)],
        out_specs=[here] * 3,
        scratch_shapes=scratch,
        compiler_params=pltpu.CompilerParams(
            collective_id=0, has_side_effects=True, vmem_limit_bytes=62 * 2**20
        ),
        cost_estimate=pl.CostEstimate(flops=flops, bytes_accessed=2**23, transcendentals=2**20),
        name="synthesis_step",
    )(*operands)


def adam_update(weight, moment, second, gradient, factor):
    clipped = gradient * factor
    moment_new = BETA_FIRST * moment + (1.0 - BETA_FIRST) * clipped
    second_new = BETA_SECOND * second + (1.0 - BETA_SECOND) * clipped * clipped
    moment_hat = moment_new / (1.0 - BETA_FIRST**STEP)
    second_hat = second_new / (1.0 - BETA_SECOND**STEP)
    weight_new = weight - LEARN_RATE * (
        moment_hat / (jnp.sqrt(second_hat) + ADAM_EPSILON) + DECAY_RATE * weight
    )
    return (moment_new, second_new, weight_new)


def adam_kernel(
    s,
    grad,
    sums,
    norm,
    conv_w,
    conv_m,
    conv_v,
    chan_w,
    chan_m,
    chan_v,
    rgb_w,
    rgb_m,
    rgb_v,
    loss_out,
    norm_out,
    conv_m_out,
    conv_v_out,
    conv_w_out,
    conv_low_out,
    chan_m_out,
    chan_v_out,
    chan_w_out,
    rgb_m_out,
    rgb_v_out,
    rgb_w_out,
    rgb_low_out,
):
    factor = jnp.minimum(1.0, CLIP_LIMIT / (norm[0:1, 0:1] + 1e-06))
    moment, second, weight = adam_update(
        conv_w[...], conv_m[...], conv_v[...], grad[...].astype(F32), factor[None]
    )
    conv_m_out[...] = moment
    conv_v_out[...] = second
    conv_w_out[...] = weight
    conv_low_out[...] = weight.astype(BF16)

    @pl.when(pl.program_id(0) == 0)
    def _():
        loss_out[0] = sums[2, 0]
        norm_out[0] = norm[0, 0]
        moment, second, weight = adam_update(
            chan_w[...], chan_m[...], chan_v[...], sums[0:2, : s.ch], factor
        )
        chan_m_out[...] = moment
        chan_v_out[...] = second
        chan_w_out[...] = weight
        moment, second, weight = adam_update(
            rgb_w[...], rgb_m[...], rgb_v[...], sums[8:11, : s.ch], factor
        )
        rgb_m_out[...] = moment
        rgb_v_out[...] = second
        rgb_w_out[...] = weight
        rgb_low_out[...] = weight.astype(BF16)


def run_adam(s, *operands):
    steps = 3
    taps = pl.BlockSpec((TAPS // steps, s.ch, s.width), lambda i: (i, 0, 0))

    def small(shape):
        return pl.BlockSpec(shape, lambda i: (0, 0))

    scalar = pl.BlockSpec(memory_space=pltpu.SMEM)
    conv = jax.ShapeDtypeStruct((TAPS, s.ch, s.width), F32)
    chan = jax.ShapeDtypeStruct((2, s.ch), F32)
    rgb = jax.ShapeDtypeStruct((3, s.ch), F32)
    one = jax.ShapeDtypeStruct((1,), F32)
    return pl.pallas_call(
        functools.partial(adam_kernel, s),
        grid=(steps,),
        out_shape=(one, one)
        + (conv,) * 3
        + (jax.ShapeDtypeStruct(conv.shape, BF16),)
        + (chan,) * 3
        + (rgb,) * 3
        + (jax.ShapeDtypeStruct(rgb.shape, BF16),),
        in_specs=[taps, small((16, LANES)), small((8, LANES))]
        + [taps] * 3
        + [small((2, s.ch))] * 3
        + [small((3, s.ch))] * 3,
        out_specs=[scalar, scalar] + [taps] * 4 + [small((2, s.ch))] * 3 + [small((3, s.ch))] * 4,
        compiler_params=pltpu.CompilerParams(vmem_limit_bytes=62 * 2**20),
        name="optimizer_step",
    )(*operands)


def local(
    mesh_shape,
    features,
    styles,
    noise_field,
    noise_keep,
    path_noise,
    length_mean,
    conv_weight,
    conv_moment,
    conv_second,
    chan_params,
    chan_moment,
    chan_second,
    rgb_weight,
    rgb_moment,
    rgb_second,
):
    s = Sizes(mesh_shape, features.shape, conv_weight.shape)
    taps_first = functools.partial(jnp.transpose, axes=(1, 0, 2))
    weight = taps_first(conv_weight)
    grad, sums, norm = run_kernel(
        s,
        features,
        styles,
        weight,
        chan_params,
        rgb_weight,
        path_noise,
        noise_field,
        noise_keep,
        length_mean,
    )
    outs = run_adam(
        s,
        grad,
        sums,
        norm,
        weight,
        taps_first(conv_moment),
        taps_first(conv_second),
        chan_params,
        chan_moment,
        chan_second,
        rgb_weight,
        rgb_moment,
        rgb_second,
    )
    return outs[:2] + tuple(taps_first(x) for x in outs[2:6]) + outs[6:]


def solution(mesh):
    whole, line = P(), P("mp", None, None)
    row, pixels = P(None, "mp"), P(None, "dp")
    in_specs = (
        P("mp", None, "dp"),
        row,
        pixels,
        pixels,
        P(None, None, "dp"),
        whole,
        line,
        line,
        line,
    ) + (row,) * 6
    out_specs = (whole, whole) + (line,) * 4 + (row,) * 7
    return jax.shard_map(
        functools.partial(local, dict(mesh.shape)),
        mesh=mesh,
        in_specs=in_specs,
        out_specs=out_specs,
        check_vma=False,
    )
```

time: 157 us -> 133 us (0.85)
  local copies, waits for them, and re-layouts: 9.92 us -> 0 us
  other arithmetic: 7.61 us -> 0 us
  Pallas kernels: 137 us -> 131 us
    pallas_call x1, Pallas kernels: 137 us -> 125 us  [run_kernel(): pl.pallas_call(functools.partial(kernel, s), out_shape=(jax.ShapeDtypeStr...]
    pallas_call x0 -> x1, Pallas kernels: none -> 6.12 us  [run_adam(): pl.pallas_call(functools.partial(adam_kernel, s), grid=(steps,), out_shap...]
    transpose x1 -> x0, other arithmetic: 4.73 us -> none  [local(): taps_first(conv_new.astype(BF16))]
    concatenate x2 -> x0, local copies, waits for them, and re-layouts: 2.51 us -> none  [the longest x1 1.77 us: local(): jnp.concatenate([path, block_order(noise, s)[:, None], blank((s.images, 4...]
    reshape x7 -> x0, local copies, waits for them, and re-layouts: 2.43 us -> none  [the longest x4 1.41 us: block_order(): x = x.reshape(lead + (2, s.px // (2 * SIDE), SIDE))]
    broadcast_in_dim x7 -> x0, local copies, waits for them, and re-layouts: 1.74 us -> none  [the longest x1 0.99 us: local(): jnp.broadcast_to(styles.T[:, :, None], (s.ch, s.images, LANES))]
    slice x2 -> x0, local copies, waits for them, and re-layouts: 1.7 us -> none  [the longest x1 1.19 us: local(): grad_norm = norm[0, 0]]
where the time goes in v2:
time: 133 us
  Pallas kernels  131 us (98%)
  between operations  1.46 us (1%)
    pallas_call x1, Pallas kernels, run_kernel(): pl.pallas_call(functools.partial(kernel, s), out_shape=(jax.ShapeDtypeStr...  125 us
    pallas_call x1, Pallas kernels, run_adam(): pl.pallas_call(functools.partial(adam_kernel, s), grid=(steps,), out_shap...  6.12 us

profile of v2, /device:TPU:0, one launch (start us, length us, event | category | flops | bytes accessed | tf_op | source)
XLA Modules:
  0.0 132.7 jit_solution(10740768729793499941)
XLA Ops:
  1.3 125.1 %synthesis_step.1 = (bf16[9,64,512]{2,1,0:T(8,128)(2,1)}, f32[16,128]{1,0:T(8,128)}, f32[8,128]{1,0:T(8,128)}) custom-call(bf16[64,16,1024]{2,1,0:T(8,128)(2,1)} %feat_hbm.1, f32[16,64]{1,0:T(8,128)} %styles.1, f32[9,64,512]{2,1,0:T(8,128)} %bitcast.7, f32[2,64]{1,0:T(2,128)} %chan_w.1, f32[3,64]{1,0:T(4,128)} %rgb_w.1, bf16[3,16,1024]{2,1,0:T(8,128)(2,1)} %path_hbm.1, ...), custom_call_target="tpu_custom_call" | custom-call | flops 19327352832 | bytes 8388608 | tf_op jit(solution)/shard_map/synthesis_step/pallas_call | solution.py:823
  126.4 6.1 %optimizer_step.1 = (f32[1]{0:T(128)}, f32[1]{0:T(128)}, f32[9,64,512]{2,1,0:T(8,128)}, f32[9,64,512]{2,1,0:T(8,128)}, f32[9,64,512]{2,1,0:T(8,128)}, /*index=5*...) custom-call(bf16[9,64,512]{2,1,0:T(8,128)(2,1)} %get-tuple-element.2, ...), custom_call_target="tpu_custom_call" | custom-call | tf_op jit(solution)/shard_map/optimizer_step/pallas_call | solution.py:921

commit v3 on v2

--- a/solution.py
+++ b/solution.py
@@ -41,8 +41,8 @@
         self.split = (self.ch // self.dp) % 16 == 0
         self.shares = self.dp if self.split else 1
         self.rows = self.ch // self.shares
-        self.taps_each = 3
-        self.first = 6
+        self.first = 7
+        self.part = 3
         self.bits = []
         bit = self.chips // 2
         while bit >= 1:
@@ -117,13 +117,13 @@
     wide_sum,
     narrow_in,
     final,
-    gathered,
     small_own,
     small_plane,
     small_mid,
     small_line,
     small_sum,
-    square_all,
+    square_near,
+    square_line,
     in_sem,
     w_send,
     w_recv,
@@ -144,7 +144,7 @@
     g_sem,
     sp_sem,
     sl_sem,
-    n_sem,
+    q_sem,
 ):
     d = lax.axis_index("dp")
     m = lax.axis_index("mp")
@@ -429,36 +429,43 @@
         lateral(q, 0)
         lateral(q, s.blocks + 1)
 
-    def convolve_math(q):
-        projected = jnp.zeros((16, s.half), F32)
-        wide = 2 * LANES
-        for p in range(0, s.px, wide):
-            acc = jnp.zeros((s.half, wide), F32)
-            for a in range(3):
-                for b in range(3):
-                    k = 3 * a + b
-                    acc += jnp.dot(
-                        weights_t[:, k * s.width : (k + 1) * s.width],
-                        grids[q, b, :, a * LANES + p : a * LANES + p + wide],
-                        preferred_element_type=F32,
-                    )
-            acts = []
-            for t in range(2):
-                cut = slice(p + t * LANES, p + (t + 1) * LANES)
-                conv = acc[:, t * LANES : (t + 1) * LANES] * conv_gain
-                noise = aux[q, :, cut].astype(F32)[3:4]
-                pre = conv * demod_cols[q] + chan_cols[1] * noise + chan_cols[0]
-                sig = jax.nn.sigmoid(pre)
-                act = pre * sig
-                scaled[q, :, cut] = conv
-                slope_of[q, :, cut] = sig * (1.0 + pre * (1.0 - sig))
-                acts.append(act.astype(BF16))
-            act = jnp.concatenate(acts, axis=1)
-            projected += lax.dot_general(aux[q, :, p : p + wide], act, NT, preferred_element_type=F32)
-        proj_all[q, place] = projected[:8]
-
-    def convolve(q):
-        convolve_math(q)
+    def blocks_of(ref, first, second):
+        if second == first + 1:
+            return ref[:, first * LANES : (second + 1) * LANES]
+        return jnp.concatenate([ref[:, j * LANES : (j + 1) * LANES] for j in (first, second)], axis=1)
+
+    def convolve(q, first, second):
+        acc = jnp.zeros((s.half, 2 * LANES), F32)
+        for a in range(3):
+            for b in range(3):
+                k = 3 * a + b
+                acc += jnp.dot(
+                    weights_t[:, k * s.width : (k + 1) * s.width],
+                    blocks_of(grids.at[q, b], first + a, second + a),
+                    preferred_element_type=F32,
+                )
+        acts = []
+        for t, j in enumerate((first, second)):
+            cut = slice(j * LANES, (j + 1) * LANES)
+            conv = acc[:, t * LANES : (t + 1) * LANES] * conv_gain
+            noise = aux[q, :, cut].astype(F32)[3:4]
+            pre = conv * demod_cols[q] + chan_cols[1] * noise + chan_cols[0]
+            sig = jax.nn.sigmoid(pre)
+            act = pre * sig
+            scaled[q, :, cut] = conv
+            slope_of[q, :, cut] = sig * (1.0 + pre * (1.0 - sig))
+            acts.append(act.astype(BF16))
+        act = jnp.concatenate(acts, axis=1)
+        return lax.dot_general(blocks_of(aux.at[q], first, second), act, NT, preferred_element_type=F32)[:8]
+
+    def convolve_inner(q):
+        projected = jnp.zeros((8, s.half), F32)
+        for j in range(1, s.blocks - 1, 2):
+            projected += convolve(q, j, j + 1)
+        proj_all[q, place] = projected
+
+    def convolve_border(q):
+        proj_all[q, place] += convolve(q, 0, s.blocks - 1)
         for dd, mm in near:
             at = proj_all.at[q, place]
             copy_to(at, at, j_send.at[q], j_recv.at[q], dd, mm).start()
@@ -524,7 +531,6 @@
     take_line(0)
     take_mate(0)
     inner(0)
-    border(0)
 
     taken(weights.at[:, pl.ds(0, s.ch), :], w_recv.at[len(s.bits)])
     if s.split:
@@ -543,42 +549,43 @@
     for q in range(s.group):
         demod_cols[q] = jnp.broadcast_to(demod_t[:, q : q + 1], (s.half, LANES))
 
-    def add_taps(q, taps):
-        for k in taps:
+    def add_taps(q):
+        for k in range(TAPS):
             total[k] += tap_grad(q, k)
 
     def stage(q, carry):
-        convolve(q)
+        border(q)
+        convolve_border(q)
+
+        @pl.when(q == last - 1)
+        def _():
+            if last > 1:
+                add_taps(q - 1)
+            signal_back(q)
+
         take_line(q + 1)
 
-        @pl.when(q > 0)
+        @pl.when(lax.rem(q, last - 1) > 0)
         def _():
-            add_taps(q - 1, range(TAPS // 2))
+            add_taps(q - 1)
 
         take_mate(q + 1)
-
-        @pl.when(q > 0)
+        inner(q + 1)
+        convolve_inner(q + 1)
+
+        @pl.when(q < last - 1)
         def _():
-            add_taps(q - 1, range(TAPS // 2, TAPS))
-
-        signal_back(q)
-        inner(q + 1)
-        border(q + 1)
+            signal_back(q)
+
         return carry
 
+    convolve_inner(0)
     lax.fori_loop(0, last, stage, 0)
 
-    convolve(last)
-    add_taps(last - 1, range(TAPS))
+    border(last)
+    convolve_border(last)
+    add_taps(last - 1)
     signal_back(last)
-    small_own[0:1] = jnp.sum(chan_acc[0].T, axis=0, keepdims=True)
-    small_own[1:2] = jnp.sum(chan_acc[1].T, axis=0, keepdims=True)
-    small_own[2:3] = loss_acc[...]
-    small_own[3:8] = jnp.zeros((5, s.half), F32)
-    small_own[8:16] = rgb_acc[...]
-    small_plane[place] = small_own[...]
-    for dd, mm in near:
-        copy_to(small_own, small_plane.at[place], sp_sem.at[0], sp_sem.at[1], dd, mm).start()
     cross = 2.0 * jnp.dot(
         columns[...] * columns[...], stat_rows[...], precision=HIGHEST, preferred_element_type=F32
     )
@@ -635,32 +642,41 @@
     def byte_count():
         return weights.at[:, pl.ds(0, len(targets) * s.rows), :]
 
-    def finish(first_tap):
-        for k in range(first_tap, first_tap + s.taps_each):
-            if k < s.first:
-                taken(line_in.at[pl.ds(1, s.chips - 1), k], l_recv.at[k])
-                acc = line_out[z, k].astype(F32)
-                for r in range(1, s.chips):
-                    acc = acc + line_in[r, k].astype(F32)
-            else:
-                b = k - s.first
-                taken(narrow_in.at[pl.ds(0, s.dp - 1), b], n_recv.at[b])
-                acc = by_shares(wide_sum[b, :, own_rows, :].astype(F32), [narrow_in[dd, b] for dd in range(s.dp)])
-            final[:, k] = acc.astype(BF16)
-            gathered[k, own_rows, own_cols] = final[c, k]
-        taps = pl.ds(first_tap, s.taps_each)
+    def finish(k, squares):
+        if k < s.first:
+            taken(line_in.at[pl.ds(1, s.chips - 1), k], l_recv.at[k])
+            acc = line_out[z, k].astype(F32)
+            for r in range(1, s.chips):
+                acc = acc + line_in[r, k].astype(F32)
+        else:
+            b = k - s.first
+            taken(narrow_in.at[pl.ds(0, s.dp - 1), b], n_recv.at[b])
+            acc = by_shares(wide_sum[b, :, own_rows, :].astype(F32), [narrow_in[dd, b] for dd in range(s.dp)])
+        final[:, k] = acc.astype(BF16)
+        kept = final[:, k].astype(F32)
+        return squares + jnp.sum(kept * kept, axis=0)
+
+    def hand_out(first_tap, count):
+        taps = pl.ds(first_tap, count)
+        there = grad_out.at[taps, own_rows, own_cols]
         for dd, mm in targets:
-            copy_to(
-                final.at[lax.rem(mm, 2), taps],
-                gathered.at[taps, own_rows, own_cols],
-                g_sem.at[0],
-                g_sem.at[1],
-                dd,
-                mm,
-            ).start()
-
-    for k in (0, 6, 1, 2, 7, 3, 4, 8, 5):
+            copy_to(final.at[lax.rem(mm, 2), taps], there, g_sem.at[0], g_sem.at[1], dd, mm).start()
+        pltpu.make_async_copy(final.at[c, taps], there, g_sem.at[2]).start()
+
+    def send_small():
+        small_own[0:1] = jnp.sum(chan_acc[0].T, axis=0, keepdims=True)
+        small_own[1:2] = jnp.sum(chan_acc[1].T, axis=0, keepdims=True)
+        small_own[2:3] = loss_acc[...]
+        small_own[3:8] = jnp.zeros((5, s.half), F32)
+        small_own[8:16] = rgb_acc[...]
+        small_plane[place] = small_own[...]
+        for dd, mm in near:
+            copy_to(small_own, small_plane.at[place], sp_sem.at[0], sp_sem.at[1], dd, mm).start()
+
+    for index, k in enumerate((0, 7, 1, 2, 3, 8, 4, 5, 6)):
         last_tap(k)
+        if index == 1:
+            send_small()
 
     taken(small_plane.at[pl.ds(0, 2 * s.dp - 1)], sp_sem.at[1])
     for h in range(2):
@@ -674,18 +690,26 @@
     for r in range(1, s.chips):
         copy_to(small_mid, small_line.at[z], sl_sem.at[0], sl_sem.at[1], d, 2 * z_at(r) + c).start()
 
+    squares = jnp.zeros((s.rows, s.half), F32)
     plane_done(0)
+    plane_done(1)
     line_done(0)
-    plane_done(1)
     plane_done(2)
+    plane_done(3)
     line_done(1)
-    plane_done(3)
-    finish(0)
     plane_done(4)
-    line_done(2)
+    for k in (0, 1, 2):
+        squares = finish(k, squares)
+    hand_out(0, 3)
     plane_done(5)
-    finish(6)
-    finish(3)
+    plane_done(6)
+    for k in (7, 8, 3, 4, 5, 6):
+        squares = finish(k, squares)
+    square_near[place] = jnp.broadcast_to(jnp.sum(squares, keepdims=True), (8, LANES))
+    for dd, mm in near:
+        at = square_near.at[place]
+        copy_to(at, at, q_sem.at[0], q_sem.at[1], dd, mm).start()
+    hand_out(3, TAPS - 3)
     taken(small_line.at[pl.ds(0, s.chips - 1)], sl_sem.at[1])
     sums = small_line[0]
     for zz in range(1, s.chips):
@@ -698,20 +722,21 @@
     mine = small_sum[lax.div(start, s.half), :, pl.ds(block, LANES)]
     small_out[...] = pltpu.roll(mine, lax.rem(2 * LANES - lax.rem(first, LANES), LANES), 1)
 
+    taken(square_near.at[pl.ds(0, 2 * s.dp - 1)], q_sem.at[1])
+    acc = square_near[0]
+    for at in range(1, 2 * s.shares):
+        acc = acc + square_near[at]
+    square_line[z] = acc
+    for r in range(1, s.chips):
+        at = square_line.at[z]
+        copy_to(at, at, q_sem.at[2], q_sem.at[3], d, 2 * z_at(r) + c).start()
+    taken(square_line.at[pl.ds(0, s.chips - 1)], q_sem.at[3])
+    acc = square_line[0]
+    for zz in range(1, s.chips):
+        acc = acc + square_line[zz]
+    norm_out[...] = jnp.sqrt(acc + chan_squares)
     taken(byte_count(), g_sem.at[1])
-    acc = jnp.zeros((s.ch, s.width), F32)
-    for k in range(TAPS):
-        grad = gathered[k].astype(F32)
-        acc = acc + grad * grad
-    square_all[m] = jnp.broadcast_to(jnp.sum(acc, keepdims=True), (8, LANES))
-    for dd, mm in line:
-        copy_to(square_all.at[m], square_all.at[m], n_sem.at[0], n_sem.at[1], dd, mm).start()
-    grad_out[...] = gathered[...]
-    taken(square_all.at[pl.ds(0, s.mp - 1)], n_sem.at[1])
-    acc = square_all[0]
-    for mm in range(1, s.mp):
-        acc = acc + square_all[mm]
-    norm_out[...] = jnp.sqrt(acc + chan_squares)
+    pltpu.make_async_copy(final.at[c], grad_out.at[:, own_rows, own_cols], g_sem.at[2]).wait()
 
     gone(weights.at[:, pl.ds(0, sent_rows), :], w_send.at[0])
     if s.split:
@@ -727,7 +752,8 @@
     gone(wide_in.at[pl.ds(1, s.chips - 1)], l_send.at[1])
     gone(narrow_in.at[pl.ds(0, s.dp - 1)], r_send.at[1])
     gone(byte_count(), g_sem.at[0])
-    gone(square_all.at[pl.ds(0, s.mp - 1)], n_sem.at[0])
+    gone(square_near.at[pl.ds(0, 2 * s.dp - 1)], q_sem.at[0])
+    gone(square_line.at[pl.ds(0, s.chips - 1)], q_sem.at[2])
 
     @pl.when(d > 0)
     def _():
@@ -789,13 +815,13 @@
         vm((rest, 2, s.ch, s.half), BF16),
         vm((s.dp, rest, 2, s.rows, s.half), BF16),
         vm((2, TAPS, s.rows, s.half), BF16),
-        vm((TAPS, s.ch, s.width), BF16),
         vm((16, s.half), F32),
         vm((2 * s.dp, 16, s.half), F32),
         vm((2, 16, s.half), F32),
         vm((s.chips, 2, 16, s.half), F32),
         vm((2, 16, s.half), F32),
-        vm((s.mp, 8, LANES), F32),
+        vm((2 * s.dp, 8, LANES), F32),
+        vm((s.chips, 8, LANES), F32),
         dma((5,)),
         dma((2,)),
         dma((len(s.bits) + 2,)),
@@ -813,10 +839,10 @@
         dma((s.first,)),
         dma((rest,)),
         dma((rest,)),
+        dma((3,)),
         dma((2,)),
         dma((2,)),
-        dma((2,)),
-        dma((2,)),
+        dma((4,)),
     ]
     flops = 2 * 2 * s.group * s.px * s.half * s.width * TAPS
     here, there = pl.BlockSpec(memory_space=pltpu.VMEM), pl.BlockSpec(memory_space=pl.ANY)
@@ -852,12 +878,12 @@
 
 def adam_kernel(
     s,
-    grad,
+    grad_hbm,
     sums,
     norm,
-    conv_w,
-    conv_m,
-    conv_v,
+    conv_w_hbm,
+    conv_m_hbm,
+    conv_v_hbm,
     chan_w,
     chan_m,
     chan_v,
@@ -877,61 +903,90 @@
     rgb_v_out,
     rgb_w_out,
     rgb_low_out,
+    grad,
+    conv_w,
+    conv_m,
+    conv_v,
+    conv_low,
+    get_sem,
+    put_sem,
 ):
+    def cut(part):
+        return pl.ds(part * s.part, s.part)
+
+    def get(part):
+        pairs = ((grad_hbm, grad), (conv_w_hbm, conv_w), (conv_m_hbm, conv_m), (conv_v_hbm, conv_v))
+        return [
+            pltpu.make_async_copy(src.at[cut(part)], dst.at[cut(part)], get_sem.at[part, j])
+            for j, (src, dst) in enumerate(pairs)
+        ]
+
+    def put(part):
+        pairs = ((conv_m, conv_m_out), (conv_v, conv_v_out), (conv_w, conv_w_out), (conv_low, conv_low_out))
+        return [
+            pltpu.make_async_copy(src.at[cut(part)], dst.at[cut(part)], put_sem.at[part, j])
+            for j, (src, dst) in enumerate(pairs)
+        ]
+
+    parts = TAPS // s.part
+    for part in range(parts):
+        for cp in get(part):
+            cp.start()
     factor = jnp.minimum(1.0, CLIP_LIMIT / (norm[0:1, 0:1] + 1e-06))
-    moment, second, weight = adam_update(
-        conv_w[...], conv_m[...], conv_v[...], grad[...].astype(F32), factor[None]
-    )
-    conv_m_out[...] = moment
-    conv_v_out[...] = second
-    conv_w_out[...] = weight
-    conv_low_out[...] = weight.astype(BF16)
-
-    @pl.when(pl.program_id(0) == 0)
-    def _():
-        loss_out[0] = sums[2, 0]
-        norm_out[0] = norm[0, 0]
-        moment, second, weight = adam_update(
-            chan_w[...], chan_m[...], chan_v[...], sums[0:2, : s.ch], factor
-        )
-        chan_m_out[...] = moment
-        chan_v_out[...] = second
-        chan_w_out[...] = weight
-        moment, second, weight = adam_update(
-            rgb_w[...], rgb_m[...], rgb_v[...], sums[8:11, : s.ch], factor
-        )
-        rgb_m_out[...] = moment
-        rgb_v_out[...] = second
-        rgb_w_out[...] = weight
-        rgb_low_out[...] = weight.astype(BF16)
+    loss_out[0] = sums[2, 0]
+    norm_out[0] = norm[0, 0]
+    moment, second, weight = adam_update(chan_w[...], chan_m[...], chan_v[...], sums[0:2, : s.ch], factor)
+    chan_m_out[...] = moment
+    chan_v_out[...] = second
+    chan_w_out[...] = weight
+    moment, second, weight = adam_update(rgb_w[...], rgb_m[...], rgb_v[...], sums[8:11, : s.ch], factor)
+    rgb_m_out[...] = moment
+    rgb_v_out[...] = second
+    rgb_w_out[...] = weight
+    rgb_low_out[...] = weight.astype(BF16)
+    for part in range(parts):
+        for cp in get(part):
+            cp.wait()
+        for k in range(part * s.part, (part + 1) * s.part):
+            moment, second, weight = adam_update(conv_w[k], conv_m[k], conv_v[k], grad[k].astype(F32), factor)
+            conv_m[k] = moment
+            conv_v[k] = second
+            conv_w[k] = weight
+            conv_low[k] = weight.astype(BF16)
+        for cp in put(part):
+            cp.start()
+    for part in range(parts):
+        for cp in put(part):
+            cp.wait()
 
 
 def run_adam(s, *operands):
-    steps = 3
-    taps = pl.BlockSpec((TAPS // steps, s.ch, s.width), lambda i: (i, 0, 0))
-
-    def small(shape):
-        return pl.BlockSpec(shape, lambda i: (0, 0))
-
+    here, there = pl.BlockSpec(memory_space=pltpu.VMEM), pl.BlockSpec(memory_space=pl.ANY)
     scalar = pl.BlockSpec(memory_space=pltpu.SMEM)
     conv = jax.ShapeDtypeStruct((TAPS, s.ch, s.width), F32)
     chan = jax.ShapeDtypeStruct((2, s.ch), F32)
     rgb = jax.ShapeDtypeStruct((3, s.ch), F32)
     one = jax.ShapeDtypeStruct((1,), F32)
+    parts = TAPS // s.part
     return pl.pallas_call(
         functools.partial(adam_kernel, s),
-        grid=(steps,),
         out_shape=(one, one)
         + (conv,) * 3
         + (jax.ShapeDtypeStruct(conv.shape, BF16),)
         + (chan,) * 3
         + (rgb,) * 3
         + (jax.ShapeDtypeStruct(rgb.shape, BF16),),
-        in_specs=[taps, small((16, LANES)), small((8, LANES))]
-        + [taps] * 3
-        + [small((2, s.ch))] * 3
-        + [small((3, s.ch))] * 3,
-        out_specs=[scalar, scalar] + [taps] * 4 + [small((2, s.ch))] * 3 + [small((3, s.ch))] * 4,
+        in_specs=[there, here, here] + [there] * 3 + [here] * 6,
+        out_specs=[scalar, scalar] + [there] * 4 + [here] * 7,
+        scratch_shapes=[
+            pltpu.VMEM(conv.shape, BF16),
+            pltpu.VMEM(conv.shape, F32),
+            pltpu.VMEM(conv.shape, F32),
+            pltpu.VMEM(conv.shape, F32),
+            pltpu.VMEM(conv.shape, BF16),
+            pltpu.SemaphoreType.DMA((parts, 4)),
+            pltpu.SemaphoreType.DMA((parts, 4)),
+        ],
         compiler_params=pltpu.CompilerParams(vmem_limit_bytes=62 * 2**20),
         name="optimizer_step",
     )(*operands)

time: 133 us -> 124 us (0.932)
  Pallas kernels: 131 us -> 122 us
    pallas_call x1, Pallas kernels: 125 us -> 117 us  [run_kernel(): pl.pallas_call(functools.partial(kernel, s), out_shape=(jax.ShapeDtypeStr...]
where the time goes in v3:
time: 124 us; the launch traced here: 123 us
  Pallas kernels  122 us (98%)
  between operations  1.46 us (1%)
    pallas_call x1, Pallas kernels, run_kernel(): pl.pallas_call(functools.partial(kernel, s), out_shape=(jax.ShapeDtypeStr...  117 us
    pallas_call x1, Pallas kernels, run_adam(): pl.pallas_call(functools.partial(adam_kernel, s), out_shape=(one, one) +...  5.1 us

profile of v3, /device:TPU:0, one launch (start us, length us, event | category | flops | bytes accessed | tf_op | source)
XLA Modules:
  0.0 123.4 jit_solution(9156603210506769616)
XLA Ops:
  1.3 116.8 %synthesis_step.1 = (bf16[9,64,512]{2,1,0:T(8,128)(2,1)}, f32[16,128]{1,0:T(8,128)}, f32[8,128]{1,0:T(8,128)}) custom-call(bf16[64,16,1024]{2,1,0:T(8,128)(2,1)} %feat_hbm.1, f32[16,64]{1,0:T(8,128)} %styles.1, f32[9,64,512]{2,1,0:T(8,128)} %bitcast.7, f32[2,64]{1,0:T(2,128)} %chan_w.1, f32[3,64]{1,0:T(4,128)} %rgb_w.1, bf16[3,16,1024]{2,1,0:T(8,128)(2,1)} %path_hbm.1, ...), custom_call_target="tpu_custom_call" | custom-call | flops 19327352832 | bytes 8388608 | tf_op jit(solution)/shard_map/synthesis_step/pallas_call | solution.py:849
  118.1 5.1 %optimizer_step.1 = (f32[1]{0:T(128)}, f32[1]{0:T(128)}, f32[9,64,512]{2,1,0:T(8,128)}, f32[9,64,512]{2,1,0:T(8,128)}, f32[9,64,512]{2,1,0:T(8,128)}, /*index=5*...) custom-call(bf16[9,64,512]{2,1,0:T(8,128)(2,1)} %get-tuple-element.2, ...), custom_call_target="tpu_custom_call" | custom-call | tf_op jit(solution)/shard_map/optimizer_step/pallas_call | solution.py:971

commit v4 on v3

--- a/solution.py
+++ b/solution.py
@@ -61,13 +61,9 @@
 def kernel(
     s,
     feat_hbm,
-    styles,
+    small,
     weight_hbm,
-    chan,
-    rgb,
-    path_hbm,
-    field_hbm,
-    keep_hbm,
+    pixels_hbm,
     mean,
     grad_out,
     small_out,
@@ -90,9 +86,7 @@
     demod_rows,
     demod_cols,
     chan_cols,
-    path,
-    field,
-    keep,
+    pixels,
     pixel_rows,
     aux_rows,
     aux,
@@ -180,14 +174,13 @@
 
     get_weight = pltpu.make_async_copy(weight_hbm, weight_own, in_sem.at[0])
     get_feat = pltpu.make_async_copy(feat_hbm, feat, in_sem.at[1])
-    get_path = pltpu.make_async_copy(path_hbm, path, in_sem.at[2])
-    get_field = pltpu.make_async_copy(field_hbm, field, in_sem.at[3])
-    get_keep = pltpu.make_async_copy(keep_hbm, keep, in_sem.at[4])
+    get_pixels = pltpu.make_async_copy(pixels_hbm, pixels, in_sem.at[2])
+    styles = small.at[: s.images]
+    chan = small.at[s.images : s.images + 2]
+    rgb = small.at[s.images + 2 : s.images + 5]
     get_weight.start()
     get_feat.start()
-    get_path.start()
-    get_field.start()
-    get_keep.start()
+    get_pixels.start()
     halo_in[...] = jnp.zeros_like(halo_in)
     barrier = pltpu.get_barrier_semaphore()
     for dd, mm in line + plane:
@@ -317,19 +310,14 @@
         held = held + fresh
 
     weights[:, grid_rows(m), :] = weight_low[:, :, pl.ds(pl.multiple_of(c * s.half, LANES), s.half)]
-    get_path.wait()
-    get_field.wait()
-    get_keep.wait()
+    get_pixels.wait()
     lane2 = lax.broadcasted_iota(jnp.int32, (1, LANES), 1)
     low2 = lane2 < SIDE
     for k in range(4):
         for q in range(s.blocks // 2):
             q2 = q + s.blocks // 2
             cuts = [slice(q * LANES, (q + 1) * LANES), slice(q2 * LANES, (q2 + 1) * LANES)]
-            if k < 3:
-                first, second = [path[k, :, cut].astype(F32) for cut in cuts]
-            else:
-                first, second = [field[:, cut].astype(F32) * keep[:, cut].astype(F32) for cut in cuts]
+            first, second = [pixels[k, :, cut] for cut in cuts]
             pixel_rows[k, :, 2 * q * LANES : (2 * q + 1) * LANES] = jnp.where(low2, first, swap_halves(second))
             pixel_rows[k, :, (2 * q + 1) * LANES : (2 * q + 2) * LANES] = jnp.where(low2, swap_halves(first), second)
     aux_rows[...] = jnp.zeros_like(aux_rows)
@@ -452,8 +440,8 @@
             pre = conv * demod_cols[q] + chan_cols[1] * noise + chan_cols[0]
             sig = jax.nn.sigmoid(pre)
             act = pre * sig
-            scaled[q, :, cut] = conv
-            slope_of[q, :, cut] = sig * (1.0 + pre * (1.0 - sig))
+            scaled[lax.rem(q, 2), :, cut] = conv
+            slope_of[lax.rem(q, 2), :, cut] = sig * (1.0 + pre * (1.0 - sig))
             acts.append(act.astype(BF16))
         act = jnp.concatenate(acts, axis=1)
         return lax.dot_general(blocks_of(aux.at[q], first, second), act, NT, preferred_element_type=F32)[:8]
@@ -506,10 +494,10 @@
             for t in range(2):
                 cut = slice(p + t * LANES, p + (t + 1) * LANES)
                 noise = aux[q, :, cut].astype(F32)[3:4]
-                grad = act_grad[:, t * LANES : (t + 1) * LANES] * slope_of[q, :, cut]
+                grad = act_grad[:, t * LANES : (t + 1) * LANES] * slope_of[lax.rem(q, 2), :, cut]
                 bias_part = bias_part + grad
                 strength_part = strength_part + grad * noise
-                stat_part = stat_part + grad * scaled[q, :, cut]
+                stat_part = stat_part + grad * scaled[lax.rem(q, 2), :, cut]
                 grad_conv[lax.rem(q, 2), :, cut] = (grad * back).astype(BF16)
         chan_acc[0] = bias_part
         chan_acc[1] = strength_part
@@ -550,8 +538,15 @@
         demod_cols[q] = jnp.broadcast_to(demod_t[:, q : q + 1], (s.half, LANES))
 
     def add_taps(q):
-        for k in range(TAPS):
-            total[k] += tap_grad(q, k)
+        def three(a, carry):
+            rows = pl.ds(pl.multiple_of(a * LANES, LANES), s.px)
+            for b in range(3):
+                total[3 * a + b] += lax.dot_general(
+                    grids[q, b, :, rows], grad_conv[lax.rem(q, 2)], NT, preferred_element_type=F32
+                )
+            return carry
+
+        lax.fori_loop(0, 3, three, 0)
 
     def stage(q, carry):
         border(q)
@@ -788,16 +783,14 @@
         vm((16, s.half), F32),
         vm((s.group, s.half, LANES), F32),
         vm((2, s.half, LANES), F32),
-        vm((3, s.images, s.px), BF16),
-        vm((s.images, s.px), BF16),
-        vm((s.images, s.px), jnp.int32),
+        vm((4, s.images, s.px), F32),
         vm((4, s.images, s.px), F32),
         vm((s.group, 16, s.px), F32),
         vm((s.group, 16, s.px), BF16),
         vm((s.group, 2, s.width // 2, LANES), BF16),
         vm((s.group, 2, s.width // 2, LANES), BF16),
-        vm((s.group, s.half, s.px), F32),
-        vm((s.group, s.half, s.px), F32),
+        vm((2, s.half, s.px), F32),
+        vm((2, s.half, s.px), F32),
         vm((s.group, 2 * s.dp, 8, s.half), F32),
         vm((2, 2, 8, s.half), F32),
         vm((16, s.half), F32),
@@ -822,7 +815,7 @@
         vm((2, 16, s.half), F32),
         vm((2 * s.dp, 8, LANES), F32),
         vm((s.chips, 8, LANES), F32),
-        dma((5,)),
+        dma((3,)),
         dma((2,)),
         dma((len(s.bits) + 2,)),
         dma((2,)),
@@ -853,11 +846,11 @@
             jax.ShapeDtypeStruct((16, LANES), F32),
             jax.ShapeDtypeStruct((8, LANES), F32),
         ),
-        in_specs=[there, here, there, here, here, there, there, there, pl.BlockSpec(memory_space=pltpu.SMEM)],
+        in_specs=[there, here, there, there, pl.BlockSpec(memory_space=pltpu.SMEM)],
         out_specs=[here] * 3,
         scratch_shapes=scratch,
         compiler_params=pltpu.CompilerParams(
-            collective_id=0, has_side_effects=True, vmem_limit_bytes=62 * 2**20
+            collective_id=0, has_side_effects=True, vmem_limit_bytes=53 * 2**20
         ),
         cost_estimate=pl.CostEstimate(flops=flops, bytes_accessed=2**23, transcendentals=2**20),
         name="synthesis_step",
@@ -878,12 +871,12 @@
 
 def adam_kernel(
     s,
-    grad_hbm,
+    grad,
     sums,
     norm,
-    conv_w_hbm,
-    conv_m_hbm,
-    conv_v_hbm,
+    conv_w,
+    conv_m,
+    conv_v,
     chan_w,
     chan_m,
     chan_v,
@@ -903,35 +896,23 @@
     rgb_v_out,
     rgb_w_out,
     rgb_low_out,
-    grad,
-    conv_w,
-    conv_m,
-    conv_v,
-    conv_low,
-    get_sem,
+    new_w,
+    new_m,
+    new_v,
+    new_low,
     put_sem,
 ):
     def cut(part):
         return pl.ds(part * s.part, s.part)
 
-    def get(part):
-        pairs = ((grad_hbm, grad), (conv_w_hbm, conv_w), (conv_m_hbm, conv_m), (conv_v_hbm, conv_v))
-        return [
-            pltpu.make_async_copy(src.at[cut(part)], dst.at[cut(part)], get_sem.at[part, j])
-            for j, (src, dst) in enumerate(pairs)
-        ]
-
     def put(part):
-        pairs = ((conv_m, conv_m_out), (conv_v, conv_v_out), (conv_w, conv_w_out), (conv_low, conv_low_out))
+        pairs = ((new_m, conv_m_out), (new_v, conv_v_out), (new_w, conv_w_out), (new_low, conv_low_out))
         return [
             pltpu.make_async_copy(src.at[cut(part)], dst.at[cut(part)], put_sem.at[part, j])
             for j, (src, dst) in enumerate(pairs)
         ]
 
     parts = TAPS // s.part
-    for part in range(parts):
-        for cp in get(part):
-            cp.start()
     factor = jnp.minimum(1.0, CLIP_LIMIT / (norm[0:1, 0:1] + 1e-06))
     loss_out[0] = sums[2, 0]
     norm_out[0] = norm[0, 0]
@@ -945,14 +926,12 @@
     rgb_w_out[...] = weight
     rgb_low_out[...] = weight.astype(BF16)
     for part in range(parts):
-        for cp in get(part):
-            cp.wait()
         for k in range(part * s.part, (part + 1) * s.part):
             moment, second, weight = adam_update(conv_w[k], conv_m[k], conv_v[k], grad[k].astype(F32), factor)
-            conv_m[k] = moment
-            conv_v[k] = second
-            conv_w[k] = weight
-            conv_low[k] = weight.astype(BF16)
+            new_m[k] = moment
+            new_v[k] = second
+            new_w[k] = weight
+            new_low[k] = weight.astype(BF16)
         for cp in put(part):
             cp.start()
     for part in range(parts):
@@ -976,18 +955,16 @@
         + (chan,) * 3
         + (rgb,) * 3
         + (jax.ShapeDtypeStruct(rgb.shape, BF16),),
-        in_specs=[there, here, here] + [there] * 3 + [here] * 6,
+        in_specs=[here] * 12,
         out_specs=[scalar, scalar] + [there] * 4 + [here] * 7,
         scratch_shapes=[
-            pltpu.VMEM(conv.shape, BF16),
             pltpu.VMEM(conv.shape, F32),
             pltpu.VMEM(conv.shape, F32),
             pltpu.VMEM(conv.shape, F32),
             pltpu.VMEM(conv.shape, BF16),
             pltpu.SemaphoreType.DMA((parts, 4)),
-            pltpu.SemaphoreType.DMA((parts, 4)),
         ],
-        compiler_params=pltpu.CompilerParams(vmem_limit_bytes=62 * 2**20),
+        compiler_params=pltpu.CompilerParams(vmem_limit_bytes=24 * 2**20),
         name="optimizer_step",
     )(*operands)
 
@@ -1016,13 +993,11 @@
     grad, sums, norm = run_kernel(
         s,
         features,
-        styles,
+        jnp.concatenate([styles, chan_params, rgb_weight], axis=0),
         weight,
-        chan_params,
-        rgb_weight,
-        path_noise,
-        noise_field,
-        noise_keep,
+        jnp.concatenate(
+            [path_noise.astype(F32), (noise_field.astype(F32) * noise_keep.astype(F32))[None]], axis=0
+        ),
         length_mean,
     )
     outs = run_adam(

time: 124 us -> 123 us (level)
  Pallas kernels: 122 us -> 118 us
  other arithmetic: 0 us -> 2.52 us
    pallas_call x1, Pallas kernels: 5.1 us -> 3.2 us  [run_adam(): pl.pallas_call(functools.partial(adam_kernel, s), out_shape=(one, one) +...]
    pallas_call x1, Pallas kernels: 117 us -> 115 us  [run_kernel(): pl.pallas_call(functools.partial(kernel, s), out_shape=(jax.ShapeDtypeStr...]
where the time goes in v4:
time: 123 us; the launch traced here: 122 us
  Pallas kernels  118 us (96%)
  other arithmetic  2.52 us (2%)
  between operations  1.62 us (1%)
    pallas_call x1, Pallas kernels, run_kernel(): pl.pallas_call(functools.partial(kernel, s), out_shape=(jax.ShapeDtypeStr...  115 us
    pallas_call x1, Pallas kernels, run_adam(): pl.pallas_call(functools.partial(adam_kernel, s), out_shape=(one, one) +...  3.2 us

profile of v4, /device:TPU:0, one launch (start us, length us, event | category | flops | bytes accessed | tf_op | source)
XLA Modules:
  0.0 122.5 jit_solution(3184433137773427371)
XLA Ops:
  1.3 0.7 pad_maximum_fusion.1.small
  2.0 0.8 multiply_bitcast_fusion
  2.9 0.9 convert_element_type.9
  3.8 0.0 copy-start
  3.8 0.0 copy-start.1
  3.8 0.0 copy-start.2
  3.9 0.0 copy-start.3
  3.9 0.0 copy-start.4
  3.9 0.0 copy-start.5
  3.9 0.0 copy-start.6
  3.9 0.0 copy-start.7
  3.9 0.0 copy-start.8
  3.9 115.1 %synthesis_step.1 = (bf16[9,64,512]{2,1,0:T(8,128)(2,1)S(1)}, f32[16,128]{1,0:T(8,128)S(1)}, f32[8,128]{1,0:T(8,128)S(1)}) custom-call(bf16[64,16,1024]{2,1,0:T(8,128)(2,1)} %feat_hbm.1, f32[21,64]{1,0:T(8,128)S(1)} %pad_maximum_fusion.1.small, f32[9,64,512]{2,1,0:T(8,128)} %bitcast.9, f32[4,16,1024]{2,1,0:T(8,128)S(1)} %pad_maximum_fusion.pixels_hbm, ...), custom_call_target="tpu_custom_call" | custom-call | flops 19327352832 | bytes 8388608 | tf_op jit(solution)/shard_map/synthesis_step/pallas_call | solution.py:842
  119.0 0.0 copy-done
  119.0 0.0 copy-done.1
  119.0 0.0 copy-done.2
  119.0 0.0 copy-done.3
  119.1 0.0 copy-done.4
  119.1 0.0 copy-done.5
  119.1 0.0 copy-done.6
  119.1 0.0 copy-done.7
  119.1 0.0 copy-done.8
  119.1 3.2 %optimizer_step.1 = (f32[1]{0:T(128)}, f32[1]{0:T(128)}, f32[9,64,512]{2,1,0:T(8,128)}, f32[9,64,512]{2,1,0:T(8,128)}, f32[9,64,512]{2,1,0:T(8,128)}, /*index=5*...) custom-call(bf16[9,64,512]{2,1,0:T(8,128)(2,1)S(1)} %get-tuple-eleme, ...), custom_call_target="tpu_custom_call" | custom-call | tf_op jit(solution)/shard_map/optimizer_step/pallas_call | solution.py:950
  (1 shorter events, 0.0 us)
Async XLA Ops:
  3.8 115.2 %copy-start = (f32[64,9,512]{2,0,1:T(8,128)S(1)}, f32[64,9,512]{2,0,1:T(8,128)}, u32[]{:S(2)}) copy-start(f32[64,9,512]{2,0,1:T(8,128)} %param.21) | copy-start | bytes 3538948
  3.8 115.2 %copy-start.1 = (f32[64,9,512]{2,0,1:T(8,128)S(1)}, f32[64,9,512]{2,0,1:T(8,128)}, u32[]{:S(2)}) copy-start(f32[64,9,512]{2,0,1:T(8,128)} %param.22) | copy-start | bytes 3538948
  3.8 115.2 %copy-start.2 = (f32[64,9,512]{2,0,1:T(8,128)S(1)}, f32[64,9,512]{2,0,1:T(8,128)}, u32[]{:S(2)}) copy-start(f32[64,9,512]{2,0,1:T(8,128)} %param.23) | copy-start | bytes 3538948
  3.9 115.2 %copy-start.3 = (f32[3,64]{1,0:T(4,128)S(1)}, f32[3,64]{1,0:T(4,128)}, u32[]{:S(2)}) copy-start(f32[3,64]{1,0:T(4,128)} %rgb_w.1) | copy-start | bytes 2308
  3.9 115.2 %copy-start.4 = (f32[2,64]{1,0:T(2,128)S(1)}, f32[2,64]{1,0:T(2,128)}, u32[]{:S(2)}) copy-start(f32[2,64]{1,0:T(2,128)} %chan_w.1) | copy-start | bytes 1540
  3.9 115.2 %copy-start.5 = (f32[3,64]{1,0:T(4,128)S(1)}, f32[3,64]{1,0:T(4,128)}, u32[]{:S(2)}) copy-start(f32[3,64]{1,0:T(4,128)} %rgb_m.1) | copy-start | bytes 2308
  3.9 115.2 %copy-start.6 = (f32[3,64]{1,0:T(4,128)S(1)}, f32[3,64]{1,0:T(4,128)}, u32[]{:S(2)}) copy-start(f32[3,64]{1,0:T(4,128)} %rgb_v.1) | copy-start | bytes 2308
  3.9 115.2 %copy-start.7 = (f32[2,64]{1,0:T(2,128)S(1)}, f32[2,64]{1,0:T(2,128)}, u32[]{:S(2)}) copy-start(f32[2,64]{1,0:T(2,128)} %chan_m.1) | copy-start | bytes 1540
  3.9 115.2 %copy-start.8 = (f32[2,64]{1,0:T(2,128)S(1)}, f32[2,64]{1,0:T(2,128)}, u32[]{:S(2)}) copy-start(f32[2,64]{1,0:T(2,128)} %chan_v.1) | copy-start | bytes 1540

commit v5 on v4

--- a/solution.py
+++ b/solution.py
@@ -185,17 +185,6 @@
     barrier = pltpu.get_barrier_semaphore()
     for dd, mm in line + plane:
         pl.semaphore_signal(barrier, inc=1, device_id=(dd, mm), device_id_type=MESH)
-    pack[...] = jnp.zeros_like(pack)
-    rgb_low[...] = rgb[...].astype(BF16)
-    rgb_eff = rgb_low[...].astype(F32) * rgb_gain
-    for zz in range(s.chips):
-        pack[zz, : s.group, : s.ch] = styles[zz * s.group : (zz + 1) * s.group, :]
-        pack[zz, s.group : s.group + 2, : s.ch] = chan[...]
-        pack[zz, 8:11, : s.ch] = rgb_eff
-    pack_all[m] = pack[z]
-    for i in range(s.ch):
-        style_cols[i] = jnp.broadcast_to(styles[:, i : i + 1], (s.images, LANES))
-
     get_weight.wait()
     for k in range(TAPS):
         weight_low[k] = weight_own[k].astype(BF16)
@@ -229,6 +218,17 @@
         mate,
     ).start()
     sent_rows += s.ch
+    pack[...] = jnp.zeros_like(pack)
+    rgb_low[...] = rgb[...].astype(BF16)
+    rgb_eff = rgb_low[...].astype(F32) * rgb_gain
+    for zz in range(s.chips):
+        pack[zz, : s.group, : s.ch] = styles[zz * s.group : (zz + 1) * s.group, :]
+        pack[zz, s.group : s.group + 2, : s.ch] = chan[...]
+        pack[zz, 8:11, : s.ch] = rgb_eff
+    pack_all[m] = pack[z]
+    for i in range(s.ch):
+        style_cols[i] = jnp.broadcast_to(styles[:, i : i + 1], (s.images, LANES))
+
     for dd, mm in line:
         copy_to(pack.at[lax.div(mm, 2)], pack_all.at[m], p_sem.at[0], p_sem.at[1], dd, mm).start()
 

time: 123 us -> 123 us (level)
  no operation moved by 1% of the time
where the time goes in v5:
time: 123 us; the launch traced here: 122 us
  Pallas kernels  118 us (96%)
  other arithmetic  2.52 us (2%)
  between operations  1.62 us (1%)
    pallas_call x1, Pallas kernels, run_kernel(): pl.pallas_call(functools.partial(kernel, s), out_shape=(jax.ShapeDtypeStr...  115 us
    pallas_call x1, Pallas kernels, run_adam(): pl.pallas_call(functools.partial(adam_kernel, s), out_shape=(one, one) +...  3.2 us

profile of v5, /device:TPU:0, one launch (start us, length us, event | category | flops | bytes accessed | tf_op | source)
XLA Modules:
  0.0 122.5 jit_solution(13215970865642929825)
XLA Ops:
  1.3 0.7 pad_maximum_fusion.1.small
  2.0 0.8 multiply_bitcast_fusion
  2.9 0.9 convert_element_type.9
  3.8 0.0 copy-start
  3.8 0.0 copy-start.1
  3.8 0.0 copy-start.2
  3.9 0.0 copy-start.3
  3.9 0.0 copy-start.4
  3.9 0.0 copy-start.5
  3.9 0.0 copy-start.6
  3.9 0.0 copy-start.7
  3.9 0.0 copy-start.8
  3.9 115.1 %synthesis_step.1 = (bf16[9,64,512]{2,1,0:T(8,128)(2,1)S(1)}, f32[16,128]{1,0:T(8,128)S(1)}, f32[8,128]{1,0:T(8,128)S(1)}) custom-call(bf16[64,16,1024]{2,1,0:T(8,128)(2,1)} %feat_hbm.1, f32[21,64]{1,0:T(8,128)S(1)} %pad_maximum_fusion.1.small, f32[9,64,512]{2,1,0:T(8,128)} %bitcast.9, f32[4,16,1024]{2,1,0:T(8,128)S(1)} %pad_maximum_fusion.pixels_hbm, ...), custom_call_target="tpu_custom_call" | custom-call | flops 19327352832 | bytes 8388608 | tf_op jit(solution)/shard_map/synthesis_step/pallas_call | solution.py:842
  119.0 0.0 copy-done
  119.0 0.0 copy-done.1
  119.0 0.0 copy-done.2
  119.1 0.0 copy-done.3
  119.1 0.0 copy-done.4
  119.1 0.0 copy-done.5
  119.1 0.0 copy-done.6
  119.1 0.0 copy-done.7
  119.1 0.0 copy-done.8
  119.1 3.2 %optimizer_step.1 = (f32[1]{0:T(128)}, f32[1]{0:T(128)}, f32[9,64,512]{2,1,0:T(8,128)}, f32[9,64,512]{2,1,0:T(8,128)}, f32[9,64,512]{2,1,0:T(8,128)}, /*index=5*...) custom-call(bf16[9,64,512]{2,1,0:T(8,128)(2,1)S(1)} %get-tuple-eleme, ...), custom_call_target="tpu_custom_call" | custom-call | tf_op jit(solution)/shard_map/optimizer_step/pallas_call | solution.py:950
  (1 shorter events, 0.0 us)
Async XLA Ops:
  3.8 115.2 %copy-start = (f32[64,9,512]{2,0,1:T(8,128)S(1)}, f32[64,9,512]{2,0,1:T(8,128)}, u32[]{:S(2)}) copy-start(f32[64,9,512]{2,0,1:T(8,128)} %param.21) | copy-start | bytes 3538948
  3.8 115.2 %copy-start.1 = (f32[64,9,512]{2,0,1:T(8,128)S(1)}, f32[64,9,512]{2,0,1:T(8,128)}, u32[]{:S(2)}) copy-start(f32[64,9,512]{2,0,1:T(8,128)} %param.22) | copy-start | bytes 3538948
  3.8 115.2 %copy-start.2 = (f32[64,9,512]{2,0,1:T(8,128)S(1)}, f32[64,9,512]{2,0,1:T(8,128)}, u32[]{:S(2)}) copy-start(f32[64,9,512]{2,0,1:T(8,128)} %param.23) | copy-start | bytes 3538948
  3.9 115.2 %copy-start.3 = (f32[3,64]{1,0:T(4,128)S(1)}, f32[3,64]{1,0:T(4,128)}, u32[]{:S(2)}) copy-start(f32[3,64]{1,0:T(4,128)} %rgb_w.1) | copy-start | bytes 2308
  3.9 115.2 %copy-start.4 = (f32[2,64]{1,0:T(2,128)S(1)}, f32[2,64]{1,0:T(2,128)}, u32[]{:S(2)}) copy-start(f32[2,64]{1,0:T(2,128)} %chan_w.1) | copy-start | bytes 1540
  3.9 115.2 %copy-start.5 = (f32[3,64]{1,0:T(4,128)S(1)}, f32[3,64]{1,0:T(4,128)}, u32[]{:S(2)}) copy-start(f32[3,64]{1,0:T(4,128)} %rgb_m.1) | copy-start | bytes 2308
  3.9 115.2 %copy-start.6 = (f32[3,64]{1,0:T(4,128)S(1)}, f32[3,64]{1,0:T(4,128)}, u32[]{:S(2)}) copy-start(f32[3,64]{1,0:T(4,128)} %rgb_v.1) | copy-start | bytes 2308
  3.9 115.2 %copy-start.7 = (f32[2,64]{1,0:T(2,128)S(1)}, f32[2,64]{1,0:T(2,128)}, u32[]{:S(2)}) copy-start(f32[2,64]{1,0:T(2,128)} %chan_m.1) | copy-start | bytes 1540
  3.9 115.2 %copy-start.8 = (f32[2,64]{1,0:T(2,128)S(1)}, f32[2,64]{1,0:T(2,128)}, u32[]{:S(2)}) copy-start(f32[2,64]{1,0:T(2,128)} %chan_v.1) | copy-start | bytes 1540
